TPU v7x, 32 devices: a whole 2x2x4 slice. The times are simulated.
32 devices in a mesh: group: 2 (over y), polar: 8 (over z, x), azimuth: 2 (over core).
Axes of the slice: x: 2, y: 2, z: 4, core: 2. Of those that a mesh axis runs over, the one named last changes fastest.
Arguments:
- state_grid: bfloat16 [768, 1440, 256], P(('group', 'polar'), 'azimuth'), parts along dimension 0, may hold values from -6 to 6
- cotangent: bfloat16 [768, 1440, 256], P(('group', 'polar'), 'azimuth'), parts along dimension 0, may hold values from -1.1953125 to 1.1953125
- legendre: bfloat16 [384, 384, 384], P('polar'), may hold values from -0.3125 to 0.3125
- quad_weight: float32 [384], replicated, may hold values from 0.3 to 3
- spec_weight: float32 [384, 2, 256], replicated, may hold values from -6 to 6
- w_in: bfloat16 [256, 512], replicated, may hold values from -0.375 to 0.375
- w_out: bfloat16 [512, 256], replicated, may hold values from -0.25 to 0.25
- lat_order: int32 [384], replicated, may hold values from 0 to 383, each once
- m_order: int32 [384], replicated, may hold values from 0 to 383, each once
Outputs:
- block_out: bfloat16 [768, 1440, 256], P(('group', 'polar'), 'azimuth'), parts along dimension 0
- spec_grad: float32 [384, 2, 512], P('polar', None, ('group', 'azimuth')), parts along dimension 2
There are 2 independent parts, one for each index of `group`. A program takes and returns all parts, laid end to end along the dimension named above; an argument that names none is the same for every part. Nothing has to cross between parts.
Inputs may be any that keep to these rules, and one draw needn't show every extreme that they name: A permutation of the latitudes: grid row i of state_grid, cotangent and block_out is latitude lat_order[i]. A permutation of the wavenumbers: row k of legendre is wavenumber m_order[k].
All inputs are finite; a program needn't handle non-finite values.
Results may differ from a plain program's by a relative error of at most 0.008.
Values may be sent and summed in bfloat16 or wider, within the bound.
A program may use at most 448 MiB of HBM per device.

v0:
```python
from functools import partial
import math

import jax
import jax.numpy as jnp
from jax import lax
from jax.sharding import PartitionSpec as P


def wave_table(m_order, lon_count):
    lon_index = jnp.arange(lon_count, dtype=jnp.int32)
    phase_int = lon_index[:, None] * m_order[None, :] % lon_count
    angle_rad = phase_int.astype(jnp.float32) * (2.0 * math.pi / lon_count)
    norm_scale = 1.0 / math.sqrt(lon_count)
    return jnp.stack(
        [jnp.cos(angle_rad) * norm_scale, -jnp.sin(angle_rad) * norm_scale], axis=1
    ).astype(jnp.bfloat16)


def rotate(coeffs, gains):
    real_part = coeffs[:, :, 0] * gains[None, :, 0] - coeffs[:, :, 1] * gains[None, :, 1]
    imag_part = coeffs[:, :, 0] * gains[None, :, 1] + coeffs[:, :, 1] * gains[None, :, 0]
    return jnp.stack([real_part, imag_part], axis=2)


def analysis(legendre_part, spectra):
    return jnp.einsum("kli,kitc->kltc", legendre_part, spectra, preferred_element_type=jnp.float32)


def synthesis(legendre_part, coefs_in):
    return jnp.einsum("kli,kltc->kitc", legendre_part, coefs_in, preferred_element_type=jnp.float32)


def local(
    state_grid, cotangent, legendre, quad_weight, spec_weight, w_in, w_out, lat_order, m_order
):
    az_count = lax.axis_size("azimuth")
    az_index = lax.axis_index("azimuth")
    polar_index = lax.axis_index("polar")
    lat_local, half_lon, channels = state_grid.shape
    full_lon = half_lon * az_count
    shard_waves = legendre.shape[0]
    degrees = legendre.shape[1]
    row_start = polar_index * lat_local
    chan_width = channels // az_count
    gain_local = lax.dynamic_slice_in_dim(spec_weight, az_index * chan_width, chan_width, 2)
    fourier_basis = wave_table(m_order, full_lon)
    row_lats = lax.dynamic_slice_in_dim(lat_order, row_start, lat_local, 0)
    row_quad = jnp.take(quad_weight, row_lats)
    waves_here = lax.dynamic_slice_in_dim(m_order, polar_index * shard_waves, shard_waves, 0)
    legendre_here = jnp.take(legendre, lat_order, axis=2)
    lower_mask = (jnp.arange(degrees, dtype=jnp.int32)[None, :] >= waves_here[:, None]).astype(
        jnp.float32
    )

    def spread(grid_in):
        pieces = grid_in.reshape(lat_local, half_lon, az_count, chan_width).transpose(2, 0, 1, 3)
        return lax.all_to_all(pieces, "azimuth", split_axis=0, concat_axis=2, tiled=True)[0]

    def to_waves(spectra):
        arrived = lax.all_to_all(spectra, "polar", split_axis=0, concat_axis=1, tiled=True)
        return arrived

    lon_full = spread(state_grid)
    fourier = jnp.einsum(
        "rnc,ntk->krtc", lon_full, fourier_basis, preferred_element_type=jnp.float32
    )
    weighted = (fourier * row_quad[None, :, None, None]).astype(jnp.bfloat16)
    at_waves = to_waves(weighted)
    coeffs = analysis(legendre_here, at_waves) * lower_mask[:, :, None, None]
    filtered = rotate(coeffs, gain_local).astype(jnp.bfloat16)
    grid_modes = synthesis(legendre_here, filtered).astype(jnp.bfloat16)
    at_rows = lax.all_to_all(grid_modes, "polar", split_axis=1, concat_axis=0, tiled=True)
    spectral = jnp.einsum(
        "krtc,ntk->rnc", at_rows, fourier_basis, preferred_element_type=jnp.float32
    ).astype(jnp.bfloat16)
    sectioned = spectral.reshape(1, lat_local, az_count, half_lon, chan_width)
    moved_back = lax.all_to_all(sectioned, "azimuth", split_axis=2, concat_axis=0, tiled=True)
    returned = (
        moved_back.reshape(az_count, lat_local, half_lon, chan_width)
        .transpose(1, 2, 0, 3)
        .reshape(lat_local, half_lon, channels)
    )
    mixed_grid = (state_grid.astype(jnp.float32) + returned.astype(jnp.float32)).astype(
        jnp.bfloat16
    )
    flat_mixed = mixed_grid.reshape(-1, channels)
    pre_act = jnp.dot(flat_mixed, w_in, preferred_element_type=jnp.float32)
    hidden, gelu_back = jax.vjp(partial(jax.nn.gelu, approximate=True), pre_act)
    block_out = (
        flat_mixed.astype(jnp.float32)
        + jnp.dot(hidden.astype(jnp.bfloat16), w_out, preferred_element_type=jnp.float32)
    ).astype(jnp.bfloat16)
    block_out = block_out.reshape(state_grid.shape)
    flat_cot = cotangent.reshape(-1, channels)
    d_hidden = jnp.dot(flat_cot, w_out.T, preferred_element_type=jnp.float32)
    d_pre = gelu_back(d_hidden)[0].astype(jnp.bfloat16)
    d_mixed = (
        flat_cot.astype(jnp.float32) + jnp.dot(d_pre, w_in.T, preferred_element_type=jnp.float32)
    ).astype(jnp.bfloat16)
    d_full = spread(d_mixed.reshape(state_grid.shape))
    d_modes = jnp.einsum(
        "rnc,ntk->krtc", d_full, fourier_basis, preferred_element_type=jnp.float32
    ).astype(jnp.bfloat16)
    d_waves = to_waves(d_modes)
    d_filt = analysis(legendre_here, d_waves)
    grad_real = jnp.sum(
        d_filt[:, :, 0] * coeffs[:, :, 0] + d_filt[:, :, 1] * coeffs[:, :, 1], axis=0
    )
    grad_imag = jnp.sum(
        d_filt[:, :, 1] * coeffs[:, :, 0] - d_filt[:, :, 0] * coeffs[:, :, 1], axis=0
    )
    grad_terms = jnp.stack([grad_real, grad_imag], axis=1)
    spec_grad = lax.psum_scatter(grad_terms, "polar", scatter_dimension=0, tiled=True)
    return (block_out, spec_grad)


def solution(mesh):
    return jax.shard_map(
        local,
        mesh=mesh,
        in_specs=(
            P(("group", "polar"), "azimuth", None),
            P(("group", "polar"), "azimuth", None),
            P("polar", None, None),
            P(),
            P(),
            P(),
            P(),
            P(),
            P(),
        ),
        out_specs=(P(("group", "polar"), "azimuth", None), P("polar", None, ("group", "azimuth"))),
        check_vma=False,
    )
```

profile of v0, /device:TPU:0, one launch (start us, length us, event | category | flops | bytes accessed | tf_op | source)
XLA Modules:
  0.0 1219.4 jit_solution(10683470110452601429)
XLA Ops:
  7.2 33.3 %reshape.157 = bf16[48,720,2,128]{3,2,1,0:T(2,128)(2,1)} reshape(bf16[48,720,256]{2,1,0:T(8,128)(2,1)} %param.9) | data formatting | bytes 35389440 | tf_op jit(solution)/shard_map/reshape | solution.py:57
  40.5 17.4 %copy.43 = bf16[2,48,720,128]{3,2,1,0:T(8,128)(2,1)} copy(bf16[2,48,720,128]{3,0,2,1:T(2,128)(2,1)} %bitcast.100) | data formatting | bytes 35389440 | tf_op jit(solution)/shard_map/transpose | solution.py:57
  58.0 10.2 all-to-all-start
  68.2 0.1 compare_select_fusion.1
  68.3 0.8 gather_fusion.1
  69.1 0.1 and_select_fusion
  69.2 13.2 %all-to-all-done = bf16[2,48,720,128]{3,2,1,0:T(8,128)(2,1)} async-done(((bf16[2,48,720,128]{3,2,1,0:T(8,128)(2,1)}), bf16[2,48,720,128]{3,2,1,0:T(8,128)(2,1)}, u32[]{:S(2)}, u32[]{:S(2)}) %all-to-all-start) | async-done | bytes 17694752 | tf_op jit(solution)/shard_map/all_to_all | solution.py:58
  82.3 8.7 copy.44
  91.0 9.6 multiply_convert_fusion.4
  100.6 17.1 %fusion.22 = bf16[384,48,2,128]{3,0,1,2:T(8,128)(2,1)} fusion(f32[48]{0:T(128)S(1)} %and_select_fusion, bf16[48,1440,128,1]{2,1,0,3:T(8,128)(2,1)S(1)} %bitcast.104, bf16[1440,1,384]{2,0,1:T(8,128)(2,1)S(1)} %get-tuple-element.9, bf16[1440,1,384]{2,0,1:T(8,128)(2,1)S(1)} %get-tuple-element.8), kind=kOutput, calls=%fused_computation.33 | convolution fusion | flops 13603405824 | bytes 29343936 | tf_op jit(solution)/shard_map/rnc,ntk->krtc/dot_general | solution.py:65
  117.7 13.3 %copy.45 = bf16[384,48,2,128]{3,1,2,0:T(8,128)(2,1)} copy(bf16[384,48,2,128]{3,0,1,2:T(8,128)(2,1)} %fusion.22) | data formatting | bytes 18874368 | tf_op jit(solution)/shard_map/convert_element_type | solution.py:68
  131.0 7.5 all-to-all-start.1
  138.5 0.1 dynamic_slice.10
  138.6 18.4 %copy.42 = bf16[48,384,384]{1,0,2:T(8,128)(2,1)} copy(bf16[48,384,384]{2,1,0:T(8,128)(2,1)} %param.11) | data formatting | bytes 28311552 | tf_op args[2]
  157.0 17.8 %gather_fusion = bf16[384,48,384]{2,1,0:T(8,128)(2,1)} fusion(bf16[48,384,384]{1,0,2:T(8,128)(2,1)} %copy.42, s32[1024]{0:T(1024)S(1)} %pad_clamp_fusion.1), kind=kCustom, calls=%fused_computation | custom fusion | bytes 28313088 | tf_op jit(solution)/shard_map/jit(_take)/gather | solution.py:51
  174.8 1.6 constant_dynamic-slice_fusion.1
  176.4 0.1 fusion.41
  176.5 13.6 %select_bitcast_fusion = bf16[48,384,384,1]{1,0,2,3:T(8,128)(2,1)} fusion(bf16[384,48,384]{2,1,0:T(8,128)(2,1)} %gather_fusion, pred[384]{0:T(512)(128)(4,1)S(1)} %compare_and_fusion), kind=kLoop, calls=%fused_computation.26 | loop fusion | flops 7077888 | bytes 28311936 | tf_op jit(solution)/shard_map/jit(_take)/select_n | solution.py:51
  190.1 154.1 %all-to-all-done.1 = bf16[384,48,2,128]{3,1,2,0:T(8,128)(2,1)} async-done(((bf16[384,48,2,128]{3,1,2,0:T(8,128)(2,1)}), bf16[384,48,2,128]{3,1,2,0:T(8,128)(2,1)}, u32[]{:S(2)}, u32[]{:S(2)}) %all-to-all-start.1) | async-done | bytes 9437216 | tf_op jit(solution)/shard_map/all_to_all | solution.py:61
  344.2 10.2 copy.46
  354.4 20.5 %broadcast_multiply_fusion = f32[48,384,2,128]{3,1,2,0:T(8,128)} fusion(f32[48,384]{1,0:T(8,128)S(1)} %fusion.41, bf16[48,384,2,128]{3,1,2,0:T(8,128)(2,1)} %bitcast.101, bf16[48,384,384,1]{1,0,2,3:T(8,128)(2,1)} %select_bitcast_fusion), kind=kOutput, calls=%fused_computation.42 | convolution fusion | flops 3628597248 | bytes 42541056 | tf_op jit(solution)/shard_map/kli,kitc->kltc/dot_general | solution.py:27
  374.9 11.7 subtract_convert_fusion
  386.6 14.7 %fusion.28 = bf16[48,384,2,128]{3,1,2,0:T(8,128)(2,1)} fusion(bf16[48,384,1,128]{3,1,2,0:T(8,128)(2,1)} %get-tuple-element.5, bf16[48,384,1,128]{3,1,2,0:T(8,128)(2,1)} %get-tuple-element.4, bf16[48,384,384,1]{1,0,2,3:T(8,128)(2,1)} %select_bitcast_fusion), kind=kOutput, calls=%fused_computation.43 | convolution fusion | flops 3647471616 | bytes 33030144 | tf_op jit(solution)/shard_map/kli,kltc->kitc/dot_general | solution.py:31
  401.3 17.5 %copy.49 = bf16[48,384,2,128]{3,2,0,1:T(2,128)(2,1)S(1)} copy(bf16[48,384,2,128]{3,1,2,0:T(8,128)(2,1)} %fusion.28) | data formatting | bytes 18874368 | tf_op jit(solution)/shard_map/convert_element_type | solution.py:72
  418.8 209.2 %all_to_all.96 = bf16[48,384,2,128]{3,2,0,1:T(2,128)(2,1)} all-to-all(bf16[48,384,2,128]{3,2,0,1:T(2,128)(2,1)S(1)} %copy.49), channel_id=1, replica_groups=mesh['group'=2,'polar'=8,'azimuth'=2] {'polar'}, dimensions={1} | all-to-all | bytes 18874368 | tf_op jit(solution)/shard_map/all_to_all | solution.py:73
  628.0 9.9 copy.50
  637.9 16.3 %bitcast_convert_fusion = bf16[1440,48,128]{2,0,1:T(8,128)(2,1)S(1)} fusion(bf16[384,48,2,128]{3,0,2,1:T(8,128)(2,1)} %bitcast.107, bf16[1440,1,384]{2,0,1:T(8,128)(2,1)S(1)} %get-tuple-element.9, bf16[1440,1,384]{2,0,1:T(8,128)(2,1)S(1)} %get-tuple-element.8), kind=kOutput, calls=%fused_computation.19 | convolution fusion | flops 13602816000 | bytes 29343744 | tf_op jit(solution)/shard_map/krtc,ntk->rnc/dot_general | solution.py:74
  654.2 8.7 copy.51
  663.0 21.0 %all_to_all.97 = bf16[1,48,2,720,128]{4,3,1,0,2:T(8,128)(2,1)S(1)} all-to-all(bf16[1,48,2,720,128]{4,3,1,0,2:T(8,128)(2,1)} %copy.51), channel_id=1, replica_groups=mesh['group'=2,'polar'=8,'azimuth'=2] {'azimuth'}, dimensions={2} | all-to-all | bytes 35389440 | tf_op jit(solution)/shard_map/all_to_all | solution.py:78
  684.0 9.1 fusion.9
  693.1 30.0 %fusion.56 = f32[34560,512]{1,0:T(8,128)} fusion(bf16[34560,256]{1,0:T(8,128)(2,1)} %bitcast.94, bf16[256,512]{1,0:T(8,128)(2,1)S(1)} %copy-done), kind=kOutput, calls=%fused_computation.83 | convolution fusion | flops 9059696640 | bytes 88735744 | tf_op jit(solution)/shard_map/dot_general | solution.py:88
  723.1 63.4 %fusion.8 = bf16[34560,256]{1,0:T(8,128)(2,1)} fusion(bf16[256,512]{1,0:T(8,128)(2,1)S(1)} %copy-done, bf16[34560,256]{1,0:T(8,128)(2,1)} %bitcast.112, f32[34560,512]{1,0:T(8,128)} %fusion.56, bf16[512,256]{1,0:T(8,128)(2,1)S(1)} %copy-done.9), kind=kOutput, calls=%fused_computation.15 | convolution fusion | flops 18499829760 | bytes 106692608 | tf_op jit(solution)/shard_map/dot_general | solution.py:99
  786.5 33.3 %reshape_reshape.3 = bf16[48,720,2,128]{3,2,1,0:T(2,128)(2,1)} reshape(bf16[34560,256]{1,0:T(8,128)(2,1)} %fusion.8) | data formatting | bytes 35389440 | tf_op jit(solution)/shard_map/reshape;reshape | solution.py:57
  819.8 10.0 copy.82
  829.7 18.1 %all_to_all.98 = bf16[2,48,720,128]{3,2,1,0:T(8,128)(2,1)S(1)} all-to-all(bf16[2,48,720,128]{3,2,1,0:T(8,128)(2,1)S(1)} %bitcast.98), channel_id=1, replica_groups=mesh['group'=2,'polar'=8,'azimuth'=2] {'azimuth'}, dimensions={0} | all-to-all | bytes 35389440 | tf_op jit(solution)/shard_map/all_to_all | solution.py:58
  847.8 6.7 copy.54
  854.6 19.6 %convert_bitcast_fusion.1 = bf16[384,48,2,128]{3,0,1,2:T(8,128)(2,1)} fusion(bf16[48,1440,128,1]{2,1,0,3:T(8,128)(2,1)} %bitcast.105, bf16[1440,1,384]{2,0,1:T(8,128)(2,1)S(1)} %copy-done.6, bf16[1440,1,384]{2,0,1:T(8,128)(2,1)S(1)} %copy-done.4), kind=kOutput, calls=%fused_computation.39 | convolution fusion | flops 13598687232 | bytes 29343744 | tf_op jit(solution)/shard_map/rnc,ntk->krtc/dot_general | solution.py:102
  874.2 13.3 %copy.55 = bf16[384,48,2,128]{3,1,2,0:T(8,128)(2,1)} copy(bf16[384,48,2,128]{3,0,1,2:T(8,128)(2,1)} %convert_bitcast_fusion.1) | data formatting | bytes 18874368 | tf_op jit(solution)/shard_map/convert_element_type | solution.py:104
  887.5 5.2 all-to-all-start.5
  892.7 0.6 dynamic-slice
  894.0 204.8 %all-to-all-done.5 = bf16[384,48,2,128]{3,1,2,0:T(8,128)(2,1)} async-done(((bf16[384,48,2,128]{3,1,2,0:T(8,128)(2,1)}), bf16[384,48,2,128]{3,1,2,0:T(8,128)(2,1)}, u32[]{:S(2)}, u32[]{:S(2)}) %all-to-all-start.5) | async-done | bytes 9437216 | tf_op jit(solution)/shard_map/all_to_all | solution.py:61
  1098.8 10.1 copy.56
  1108.9 16.7 %fusion.16 = f32[48,384,2,128]{3,1,2,0:T(8,128)} fusion(bf16[48,384,2,128]{3,1,2,0:T(8,128)(2,1)} %bitcast.102, bf16[48,384,384,1]{1,0,2,3:T(8,128)(2,1)} %select_bitcast_fusion), kind=kOutput, calls=%fused_computation.27 | convolution fusion | flops 3623878656 | bytes 42467328 | tf_op jit(solution)/shard_map/kli,kitc->kltc/dot_general | solution.py:27
  1125.6 13.6 %add_reduce_fusion = (f32[384,128]{1,0:T(8,128)S(1)}, f32[384,128]{1,0:T(8,128)S(1)}) fusion(f32[48,384,2,128]{3,1,2,0:T(8,128)} %fusion.16, f32[48,384,2,128]{3,1,2,0:T(8,128)} %broadcast_multiply_fusion), kind=kLoop, calls=%fused_computation.38 | loop fusion | flops 18776064 | bytes 38141952 | tf_op jit(solution)/shard_map/reduce_sum | solution.py:107
  1139.2 1.1 pad_maximum_fusion.4
  1140.4 40.9 %fusion.7 = bf16[34560,256]{1,0:T(8,128)(2,1)} fusion(bf16[512,256]{1,0:T(8,128)(2,1)S(1)} %copy-done.9, f32[34560,512]{1,0:T(8,128)} %fusion.56, bf16[34560,256]{1,0:T(8,128)(2,1)} %bitcast.95), kind=kOutput, calls=%fused_computation.14 | convolution fusion | flops 9245491200 | bytes 106430464 | tf_op jit(solution)/shard_map/dot_general | solution.py:92
  1181.3 29.5 %all-reduce.3.cloned.1.call-done = f32[384,2,128]{2,1,0:T(2,128)} async-done(((f32[384,2,128]{2,1,0:T(2,128)}), f32[384,2,128]{2,1,0:T(2,128)}) %all-reduce.3.cloned.1.call-update) | async-done | bytes 393232
  1210.9 1.4 constant_dynamic-slice_fusion
  (39 shorter events, 0.2 us)
Async XLA Ops:
  7.2 685.9 %copy-start = (bf16[256,512]{1,0:T(8,128)(2,1)S(1)}, bf16[256,512]{1,0:T(8,128)(2,1)}, u32[]{:S(2)}) copy-start(bf16[256,512]{1,0:T(8,128)(2,1)} %param.14) | copy-start | bytes 786436
  58.0 10.2 copy-start.7
  58.0 10.3 copy-start.2
  58.0 24.3 %all-to-all-start = ((bf16[2,48,720,128]{3,2,1,0:T(8,128)(2,1)}), bf16[2,48,720,128]{3,2,1,0:T(8,128)(2,1)}, u32[]{:S(2)}, u32[]{:S(2)}) async-start(bf16[2,48,720,128]{3,2,1,0:T(8,128)(2,1)} %copy.43), calls=%async_computation | async-start | bytes 35389440 | tf_op jit(solution)/shard_map/all_to_all | solution.py:58
  82.3 8.7 copy-start.8
  100.6 537.3 %copy-start.3 = (bf16[1440,1,384]{2,0,1:T(8,128)(2,1)}, bf16[1440,1,384]{2,0,1:T(8,128)(2,1)S(1)}, u32[]{:S(2)}) copy-start(bf16[1440,1,384]{2,0,1:T(8,128)(2,1)S(1)} %get-tuple-element.8) | copy-start | bytes 3317764
  100.6 537.3 %copy-start.5 = (bf16[1440,1,384]{2,0,1:T(8,128)(2,1)}, bf16[1440,1,384]{2,0,1:T(8,128)(2,1)S(1)}, u32[]{:S(2)}) copy-start(bf16[1440,1,384]{2,0,1:T(8,128)(2,1)S(1)} %get-tuple-element.9) | copy-start | bytes 3317764
  131.0 213.2 %all-to-all-start.1 = ((bf16[384,48,2,128]{3,1,2,0:T(8,128)(2,1)}), bf16[384,48,2,128]{3,1,2,0:T(8,128)(2,1)}, u32[]{:S(2)}, u32[]{:S(2)}) async-start(bf16[384,48,2,128]{3,1,2,0:T(8,128)(2,1)} %copy.45), calls=%async_computation.1 | async-start | bytes 18874368 | tf_op jit(solution)/shard_map/all_to_all | solution.py:61
  654.2 29.7 %slice-start = ((s8[17694720]{0:T(1024)(128)(4,1)}), s8[4194304]{0:T(1024)(128)(4,1)S(1)}, s32[]{:S(2)}) async-start(s8[17694720]{0:T(1024)(128)(4,1)} %bitcast.96), calls=%async_computation.7 | async-start | bytes 8388608
  654.2 29.7 %slice-start.1 = ((s8[17694720]{0:T(1024)(128)(4,1)}), s8[4194304]{0:T(1024)(128)(4,1)S(1)}, s32[]{:S(2)}) async-start(s8[17694720]{0:T(1024)(128)(4,1)} %bitcast.96), calls=%async_computation.8 | async-start | bytes 8388608
  654.2 29.7 %slice-start.2 = ((s8[17694720]{0:T(1024)(128)(4,1)}), s8[4194304]{0:T(1024)(128)(4,1)S(1)}, s32[]{:S(2)}) async-start(s8[17694720]{0:T(1024)(128)(4,1)} %bitcast.96), calls=%async_computation.9 | async-start | bytes 8388608
  663.0 21.0 %slice-start.3 = ((s8[17694720]{0:T(1024)(128)(4,1)}), s8[4194304]{0:T(1024)(128)(4,1)S(1)}, s32[]{:S(2)}) async-start(s8[17694720]{0:T(1024)(128)(4,1)} %bitcast.96), calls=%async_computation.10 | async-start | bytes 8388608
  663.0 21.0 %slice-start.4 = ((s8[17694720]{0:T(1024)(128)(4,1)}), s8[917504]{0:T(1024)(128)(4,1)S(1)}, s32[]{:S(2)}) async-start(s8[17694720]{0:T(1024)(128)(4,1)} %bitcast.96), calls=%async_computation.11 | async-start | bytes 1835008
  693.1 30.0 %copy-start.9 = (bf16[512,256]{1,0:T(8,128)(2,1)S(1)}, bf16[512,256]{1,0:T(8,128)(2,1)}, u32[]{:S(2)}) copy-start(bf16[512,256]{1,0:T(8,128)(2,1)} %param.15) | copy-start | bytes 786436
  847.8 6.7 copy-start.4
  847.8 6.7 copy-start.6
  887.5 5.2 copy-start.10
  887.5 211.3 %all-to-all-start.5 = ((bf16[384,48,2,128]{3,1,2,0:T(8,128)(2,1)}), bf16[384,48,2,128]{3,1,2,0:T(8,128)(2,1)}, u32[]{:S(2)}, u32[]{:S(2)}) async-start(bf16[384,48,2,128]{3,1,2,0:T(8,128)(2,1)} %copy.55), calls=%async_computation.5 | async-start | bytes 18874368 | tf_op jit(solution)/shard_map/all_to_all | solution.py:61
  892.7 318.2 %all-reduce.3.cloned.1.call-start = ((), (), s32[]{:S(2)}) async-start(), calls=%async_computation.6 | async-start | bytes 786432
  1140.4 71.9 %copy-start.1 = (bf16[256,512]{1,0:T(8,128)(2,1)S(1)}, bf16[256,512]{1,0:T(8,128)(2,1)}, u32[]{:S(2)}) copy-start(bf16[256,512]{1,0:T(8,128)(2,1)} %param.14) | copy-start | bytes 786436
Sparse Core Ops, SparseCore 0:
  1140.5 70.3 all-reduce.2
where the time goes:
time: 1230 us; the launch traced here: 1220 us
  waiting for transfers between devices  402 us (33%)
  blocking collectives  248 us (20%)
  matrix products  239 us (19%)
  local copies, waits for them, and re-layouts  233 us (19%)
  other arithmetic  59 us (5%)
  starting transfers between devices  22.9 us (2%)
  between operations  15.1 us (1%)
    all_to_all x2, waiting for transfers between devices, to_waves(): lax.all_to_all(spectra, 'polar', split_axis=0, concat_axis=1, tiled=True)  359 us
    all_to_all x1, blocking collectives, local(): lax.all_to_all(grid_modes, 'polar', split_axis=1, concat_axis=0, tiled=True)  209 us
    dot_general x1, matrix products, local(): jnp.dot(d_pre, w_in.T, preferred_element_type=jnp.float32)  63.4 us
    another operation x2, local copies, waits for them, and re-layouts, spread(): grid_in.reshape(lat_local, half_lon, az_count, chan_width)  43.3 us
    dot_general x1, matrix products, local(): jnp.dot(hidden.astype(jnp.bfloat16), w_out, preferred_element_type=jnp.fl...  40.9 us
    dot_general x2, matrix products, analysis(): jnp.einsum('kli,kitc->kltc', legendre_part, spectra, preferred_element_ty...  37.1 us
    reshape x1, local copies, waits for them, and re-layouts, spread(): grid_in.reshape(lat_local, half_lon, az_count, chan_width)  33.3 us
    dot_general x1, matrix products, local(): pre_act = jnp.dot(flat_mixed, w_in, preferred_element_type=jnp.float32)  30 us
  transfers between devices with their start and end apart: 4, of which 4 were waited for; matrix products, arithmetic and copies ran while one was open for 8% of the time, Pallas kernels for 0%

commit v1 on v0

v1 whole, which is shorter than its diff:
```python
from functools import partial
import math

import jax
import jax.numpy as jnp
from jax import lax
from jax.sharding import PartitionSpec as P


def wave_table(m_order, lon_index, lon_count):
    phase_int = lon_index[:, None] * m_order[None, :] % lon_count
    angle_rad = phase_int.astype(jnp.float32) * (2.0 * math.pi / lon_count)
    norm_scale = 1.0 / math.sqrt(lon_count)
    return jnp.stack(
        [jnp.cos(angle_rad) * norm_scale, -jnp.sin(angle_rad) * norm_scale], axis=1
    ).astype(jnp.bfloat16)


def rotate(coeffs, gains):
    real_part = coeffs[:, :, 0] * gains[None, :, 0] - coeffs[:, :, 1] * gains[None, :, 1]
    imag_part = coeffs[:, :, 0] * gains[None, :, 1] + coeffs[:, :, 1] * gains[None, :, 0]
    return jnp.stack([real_part, imag_part], axis=2)


def local(
    state_grid, cotangent, legendre, quad_weight, spec_weight, w_in, w_out, lat_order, m_order
):
    polar_count = lax.axis_size("polar")
    az_count = lax.axis_size("azimuth")
    az_index = lax.axis_index("azimuth")
    polar_index = lax.axis_index("polar")
    rows, half_lon, channels = state_grid.shape
    full_lon = half_lon * az_count
    waves = legendre.shape[0]
    degrees = legendre.shape[1]
    row_start = polar_index * rows
    width = channels // az_count
    wave_chunks = 3 if waves % 3 == 0 else 1
    row_chunks = 3 if rows % 3 == 0 else 1
    kg = waves // wave_chunks
    rg = rows // row_chunks
    swap = [(0, 1), (1, 0)]
    gain_local = lax.dynamic_slice_in_dim(spec_weight, az_index * width, width, 2)
    lon_index = (jnp.arange(full_lon, dtype=jnp.int32) + az_index * half_lon) % full_lon
    basis = wave_table(m_order, lon_index, full_lon)
    row_lats = lax.dynamic_slice_in_dim(lat_order, row_start, rows, 0)
    row_quad = jnp.take(quad_weight, row_lats)
    waves_here = lax.dynamic_slice_in_dim(m_order, polar_index * waves, waves, 0)
    lat_pick = (jnp.arange(lat_order.shape[0], dtype=jnp.int32)[:, None] == lat_order[None, :]).astype(
        jnp.bfloat16
    )
    lower_mask = (jnp.arange(degrees, dtype=jnp.int32)[None, :] >= waves_here[:, None]).astype(
        jnp.float32
    )

    def spread(grid_in):
        own = lax.dynamic_slice_in_dim(grid_in, az_index * width, width, 2)
        other = lax.dynamic_slice_in_dim(grid_in, (1 - az_index) * width, width, 2)
        return jnp.concatenate([own, lax.ppermute(other, "azimuth", swap)], axis=1)

    def exchange(x):
        return lax.all_to_all(x, "polar", split_axis=0, concat_axis=0, tiled=True)

    lon_full = spread(state_grid)
    basis_parts = basis.reshape(full_lon, 2, polar_count, wave_chunks, kg)
    table = jnp.dot(
        legendre.reshape(waves * degrees, -1), lat_pick, preferred_element_type=jnp.float32
    ).astype(jnp.bfloat16)
    table = table.reshape(waves, degrees, polar_count, rows)

    coeffs, modes = [], []
    for g in range(wave_chunks):
        fourier = jnp.einsum(
            "rnc,ntpk->pkrtc", lon_full, basis_parts[:, :, :, g], preferred_element_type=jnp.float32
        )
        weighted = (fourier * row_quad[None, None, :, None, None]).astype(jnp.bfloat16)
        at_waves = exchange(weighted)
        part = table[g * kg : (g + 1) * kg]
        mask = lower_mask[g * kg : (g + 1) * kg]
        coeffs_g = jnp.einsum(
            "klpr,pkrtc->kltc", part, at_waves, preferred_element_type=jnp.float32
        ) * mask[:, :, None, None]
        filtered = rotate(coeffs_g, gain_local).astype(jnp.bfloat16)
        modes_g = jnp.einsum(
            "klpr,kltc->pkrtc", part, filtered, preferred_element_type=jnp.float32
        ).astype(jnp.bfloat16)
        coeffs.append(coeffs_g)
        modes.append(modes_g)

    block_outs = []
    d_filt = None
    for h in range(row_chunks):
        span = slice(h * rg, (h + 1) * rg)
        at_rows = exchange(jnp.concatenate([m[:, :, span] for m in modes], axis=1))
        at_rows = at_rows.reshape(polar_count * waves, rg, 2, width)
        spectral = jnp.einsum(
            "krtc,ntk->rnc", at_rows, basis, preferred_element_type=jnp.float32
        ).astype(jnp.bfloat16)
        own = spectral[:, :half_lon]
        came = lax.ppermute(spectral[:, half_lon:], "azimuth", swap)
        returned = jnp.where(
            az_index == 0,
            jnp.concatenate([own, came], axis=2),
            jnp.concatenate([came, own], axis=2),
        )
        mixed = (state_grid[span].astype(jnp.float32) + returned.astype(jnp.float32)).astype(
            jnp.bfloat16
        )
        flat_mixed = mixed.reshape(-1, channels)
        pre_act = jnp.dot(flat_mixed, w_in, preferred_element_type=jnp.float32)
        hidden, gelu_back = jax.vjp(partial(jax.nn.gelu, approximate=True), pre_act)
        block_out = (
            flat_mixed.astype(jnp.float32)
            + jnp.dot(hidden.astype(jnp.bfloat16), w_out, preferred_element_type=jnp.float32)
        ).astype(jnp.bfloat16)
        block_outs.append(block_out.reshape(mixed.shape))
        flat_cot = cotangent[span].reshape(-1, channels)
        d_hidden = jnp.dot(flat_cot, w_out.T, preferred_element_type=jnp.float32)
        d_pre = gelu_back(d_hidden)[0].astype(jnp.bfloat16)
        d_mixed = (
            flat_cot.astype(jnp.float32)
            + jnp.dot(d_pre, w_in.T, preferred_element_type=jnp.float32)
        ).astype(jnp.bfloat16)
        d_full = spread(d_mixed.reshape(mixed.shape))
        d_modes = jnp.einsum(
            "rnc,ntk->krtc", d_full, basis, preferred_element_type=jnp.float32
        ).astype(jnp.bfloat16)
        d_waves = exchange(d_modes.reshape(polar_count, waves, rg, 2, width))
        d_part = jnp.einsum(
            "klpr,pkrtc->kltc", table[:, :, :, span], d_waves, preferred_element_type=jnp.float32
        )
        d_filt = d_part if d_filt is None else d_filt + d_part

    grad_real, grad_imag = 0.0, 0.0
    for g in range(wave_chunks):
        c, d = coeffs[g], d_filt[g * kg : (g + 1) * kg]
        grad_real += jnp.sum(d[:, :, 0] * c[:, :, 0] + d[:, :, 1] * c[:, :, 1], axis=0)
        grad_imag += jnp.sum(d[:, :, 1] * c[:, :, 0] - d[:, :, 0] * c[:, :, 1], axis=0)
    grad_terms = jnp.stack([grad_real, grad_imag], axis=1)
    shares = exchange(grad_terms.reshape(polar_count, degrees // polar_count, 2, width))
    spec_grad = jnp.sum(shares, axis=0)
    return (jnp.concatenate(block_outs, axis=0), spec_grad)


def solution(mesh):
    return jax.shard_map(
        local,
        mesh=mesh,
        in_specs=(
            P(("group", "polar"), "azimuth", None),
            P(("group", "polar"), "azimuth", None),
            P("polar", None, None),
            P(),
            P(),
            P(),
            P(),
            P(),
            P(),
        ),
        out_specs=(P(("group", "polar"), "azimuth", None), P("polar", None, ("group", "azimuth"))),
        check_vma=False,
    )
```

time: 1230 us -> 976 us (0.79)
  blocking collectives: 248 us -> 0 us
  local copies, waits for them, and re-layouts: 233 us -> 106 us
  matrix products: 239 us -> 319 us
  starting transfers between devices: 22.9 us -> 49.3 us
  other arithmetic: 59 us -> 82.3 us
  between operations: 15.1 us -> 1.8 us
    all_to_all x3 -> x0, blocking collectives: 248 us -> none  [the longest x1 209 us: local(): lax.all_to_all(grid_modes, 'polar', split_axis=1, concat_axis=0, tiled=True)]
    dot_general x6 -> x19, matrix products: 105 us -> 167 us  [the longest x3 46.7 us: local(): jnp.einsum('klpr,pkrtc->kltc', table[:, :, :, span], d_waves, preferred_e...]
    all_to_all x5 -> x0, local copies, waits for them, and re-layouts: 45.6 us -> none  [the longest x2 20.4 us: to_waves(): lax.all_to_all(spectra, 'polar', split_axis=0, concat_axis=1, tiled=True)]
    another operation x2 -> x0, local copies, waits for them, and re-layouts: 43.3 us -> none  [spread(): grid_in.reshape(lat_local, half_lon, az_count, chan_width)]
    convert_element_type x3, local copies, waits for them, and re-layouts: 44.1 us -> 7.46 us  [local(): (fourier * row_quad[None, None, :, None, None]).astype(jnp.bfloat16)]
    all_to_all x3 -> x10, waiting for transfers between devices: 372 us -> 406 us  [exchange(): return lax.all_to_all(x, 'polar', split_axis=0, concat_axis=0, tiled=True)]
    reshape x2 -> x3, local copies, waits for them, and re-layouts: 42.1 us -> 11 us  [local(): d_waves = exchange(d_modes.reshape(polar_count, waves, rg, 2, width))]
    slice x0 -> x9, local copies, waits for them, and re-layouts: none -> 30.7 us  [the longest x3 7.85 us: local(): own = spectral[:, :half_lon]]
  transfers between devices with their start and end apart: 4 -> 17, of which waited for: 4 -> 10; matrix products, arithmetic and copies ran while one was open for 8% -> 35% of each run, Pallas kernels for 0% -> 0%
where the time goes in v1:
time: 976 us; the launch traced here: 967 us
  waiting for transfers between devices  408 us (42%)
  matrix products  319 us (33%)
  local copies, waits for them, and re-layouts  106 us (11%)
  other arithmetic  82.3 us (8%)
  starting transfers between devices  49.3 us (5%)
    all_to_all x10, waiting for transfers between devices, exchange(): return lax.all_to_all(x, 'polar', split_axis=0, concat_axis=0, tiled=True)  406 us
    dot_general x3, matrix products, local(): jnp.dot(d_pre, w_in.T, preferred_element_type=jnp.float32)  75 us
    all_to_all x10, starting transfers between devices, exchange(): return lax.all_to_all(x, 'polar', split_axis=0, concat_axis=0, tiled=True)  47.8 us
    dot_general x3, matrix products, local(): jnp.einsum('klpr,pkrtc->kltc', table[:, :, :, span], d_waves, preferred_e...  46.7 us
    dot_general x3, matrix products, local(): jnp.dot(hidden.astype(jnp.bfloat16), w_out, preferred_element_type=jnp.fl...  46.3 us
    dot_general x3, matrix products, local(): pre_act = jnp.dot(flat_mixed, w_in, preferred_element_type=jnp.float32)  31.5 us
    dynamic_slice x4, local copies, waits for them, and re-layouts, spread(): own = lax.dynamic_slice_in_dim(grid_in, az_index * width, width, 2)  28.1 us
    dot_general x3, matrix products, local(): jnp.einsum('rnc,ntpk->pkrtc', lon_full, basis_parts[:, :, :, g], preferre...  26.9 us
  transfers between devices with their start and end apart: 17, of which 10 were waited for; matrix products, arithmetic and copies ran while one was open for 35% of the time, Pallas kernels for 0%

profile of v1, /device:TPU:0, one launch (start us, length us, event | category | flops | bytes accessed | tf_op | source)
XLA Modules:
  0.0 966.8 jit_solution(16012170726238586232)
XLA Ops:
  0.7 12.0 %constant_dynamic-slice_fusion.9 = (bf16[48,720,128]{2,1,0:T(8,128)(2,1)}, bf16[48,720,128]{2,1,0:T(8,128)(2,1)}) fusion(bf16[48,720,256]{2,1,0:T(8,128)(2,1)} %param.9, s32[]{:T(128)S(6)} %select_n.86, s32[]{:T(128)S(6)} %select_n.87), kind=kLoop, calls=%fused_computation.215 | loop fusion | bytes 35389448 | tf_op jit(solution)/shard_map/dynamic_slice | solution.py:57
  14.2 10.5 %multiply_convert_fusion.10 = (bf16[1440,1,8,3,16]{0,4,3,2,1:T(8,128)(2,1)S(1)}, bf16[1440,1,8,3,16]{0,4,3,2,1:T(8,128)(2,1)S(1)}) fusion(s32[8,3,16]{2,1,0:T(4,128)S(1)} %mul.438, s32[1440]{0:T(1024)S(1)} %add_select_fusion.2), kind=kLoop, calls=%fused_computation.161 | loop fusion | flops 7741440 | bytes 2219136 | tf_op jit(solution)/shard_map/convert.6
  26.9 8.9 fusion.78
  38.2 7.2 all-to-all-start.1
  45.4 9.0 fusion.77
  57.0 59.5 %all-to-all-done.1 = bf16[8,16,48,2,128]{4,2,3,1,0:T(8,128)(2,1)S(1)} async-done(((bf16[8,16,48,2,128]{4,2,3,1,0:T(8,128)(2,1)}), bf16[8,16,48,2,128]{4,2,3,1,0:T(8,128)(2,1)S(1)}, u32[]{:S(2)}, u32[]{:S(2)}) %all-to-all-start.1) | async-done | bytes 3145760 | tf_op jit(solution)/shard_map/all_to_all | solution.py:62
  121.0 9.0 fusion.79
  132.5 58.6 %all-to-all-done = bf16[8,16,48,2,128]{4,2,3,1,0:T(8,128)(2,1)} async-done(((bf16[8,16,48,2,128]{4,2,3,1,0:T(8,128)(2,1)}), bf16[8,16,48,2,128]{4,2,3,1,0:T(8,128)(2,1)}, u32[]{:S(2)}, u32[]{:S(2)}) %all-to-all-start) | async-done | bytes 3145760 | tf_op jit(solution)/shard_map/all_to_all | solution.py:62
  195.7 20.9 %convolution_convert_fusion = bf16[384,18432]{1,0:T(8,128)(2,1)} fusion(bf16[18432,384]{1,0:T(8,128)(2,1)} %bitcast.231, s32[384]{0:T(512)S(1)} %copy-done.25), kind=kOutput, calls=%fused_computation.7 | convolution fusion | flops 5443190784 | bytes 28313088 | tf_op jit(solution)/shard_map/dot_general | solution.py:66
  216.6 5.7 fusion.189
  234.9 6.4 bitcast_multiply_fusion.2
  241.3 24.6 %all-to-all-done.2 = bf16[8,16,48,2,128]{4,2,3,1,0:T(8,128)(2,1)} async-done(((bf16[8,16,48,2,128]{4,2,3,1,0:T(8,128)(2,1)}), bf16[8,16,48,2,128]{4,2,3,1,0:T(8,128)(2,1)}, u32[]{:S(2)}, u32[]{:S(2)}) %all-to-all-start.2) | async-done | bytes 3145760 | tf_op jit(solution)/shard_map/all_to_all | solution.py:62
  265.9 5.1 bitcast_multiply_fusion
  273.3 5.6 subtract_convert_fusion.2
  278.9 5.2 convert_bitcast_fusion
  306.9 66.1 %all-to-all-done.5 = bf16[8,48,16,2,128]{4,2,3,1,0:T(8,128)(2,1)} async-done(((bf16[8,48,16,2,128]{4,2,3,1,0:T(8,128)(2,1)}), bf16[8,48,16,2,128]{4,2,3,1,0:T(8,128)(2,1)}, u32[]{:S(2)}, u32[]{:S(2)}) %all-to-all-start.5) | async-done | bytes 3145760 | tf_op jit(solution)/shard_map/all_to_all | solution.py:62
  380.1 67.4 %all-to-all-done.4 = bf16[8,48,16,2,128]{4,2,3,1,0:T(8,128)(2,1)} async-done(((bf16[8,48,16,2,128]{4,2,3,1,0:T(8,128)(2,1)}), bf16[8,48,16,2,128]{4,2,3,1,0:T(8,128)(2,1)}, u32[]{:S(2)}, u32[]{:S(2)}) %all-to-all-start.4) | async-done | bytes 3145760 | tf_op jit(solution)/shard_map/all_to_all | solution.py:62
  452.4 10.5 %multiply_convert_fusion.12 = (bf16[1440,1,384]{2,0,1:T(8,128)(2,1)S(1)}, bf16[1440,1,384]{2,0,1:T(8,128)(2,1)S(1)}) fusion(s32[384]{0:T(512)S(1)} %copy-done.28, s32[1440]{0:T(1024)S(1)} %copy-done.27), kind=kLoop, calls=%fused_computation.179 | loop fusion | flops 7741440 | bytes 2219136 | tf_op jit(solution)/shard_map/convert.8
  462.9 7.9 fusion.63
  472.8 7.1 fusion.64
  482.9 39.7 %all-to-all-done.3 = bf16[8,48,16,2,128]{4,2,3,1,0:T(8,128)(2,1)} async-done(((bf16[8,48,16,2,128]{4,2,3,1,0:T(8,128)(2,1)}), bf16[8,48,16,2,128]{4,2,3,1,0:T(8,128)(2,1)}, u32[]{:S(2)}, u32[]{:S(2)}) %all-to-all-start.3) | async-done | bytes 3145760 | tf_op jit(solution)/shard_map/all_to_all | solution.py:62
  522.6 7.2 fusion.62
  533.2 10.2 %copy.140 = bf16[48,8,48,384]{3,2,1,0:T(8,128)(2,1)S(1)} copy(bf16[48,8,48,384]{3,1,2,0:T(8,128)(2,1)} %bitcast.229) | data formatting | bytes 28311552
  543.4 6.1 fusion.188
  549.6 6.7 fusion.187
  556.3 23.6 %add_convert_fusion.2 = (bf16[16,720,256]{2,1,0:T(8,128)(2,1)S(1)}, bf16[16,720,256]{2,1,0:T(8,128)(2,1)}, bf16[16,720,256]{2,1,0:T(8,128)(2,1)}) fusion(bf16[16,720,128]{2,1,0:T(8,128)(2,1)} %collective-permute-done.1, bf16[16,720,128]{2,1,0:T(8,128)(2,1)} %get-tuple-element.42, bf16[48,720,256]{2,1,0:T(8,128)(2,1)} %param.9, pred[]{:T(512)S(6)} %eq.12, ...), kind=kLoop, calls=%fused_computation.65 | loop fusion | flops 115015680 | bytes 53084160 | tf_op jit(solution)/shard_map/convert_element_type | solution.py:106
  579.9 9.6 fusion.197
  589.5 24.9 %fusion.23 = bf16[11520,256]{1,0:T(8,128)(2,1)} fusion(bf16[256,512]{1,0:T(8,128)(2,1)S(1)} %copy-done, bf16[11520,256]{1,0:T(8,128)(2,1)} %bitcast.254, f32[11520,512]{1,0:T(8,128)} %fusion.197, bf16[512,256]{1,0:T(8,128)(2,1)S(1)} %copy-done.29), kind=kOutput, calls=%fused_computation.41 | convolution fusion | flops 6166609920 | bytes 35913728 | tf_op jit(solution)/shard_map/dot_general | solution.py:122
  614.4 5.8 constant_dynamic-slice_fusion.6
  620.7 9.4 fusion.198
  630.1 24.9 %fusion.22 = bf16[11520,256]{1,0:T(8,128)(2,1)} fusion(bf16[256,512]{1,0:T(8,128)(2,1)S(1)} %copy-done, bf16[11520,256]{1,0:T(8,128)(2,1)} %bitcast.253, f32[11520,512]{1,0:T(8,128)} %fusion.198, bf16[512,256]{1,0:T(8,128)(2,1)S(1)} %copy-done.29), kind=kOutput, calls=%fused_computation.39 | convolution fusion | flops 6166609920 | bytes 35913728 | tf_op jit(solution)/shard_map/dot_general | solution.py:122
  659.8 12.5 %fusion.199 = f32[11520,512]{1,0:T(8,128)} fusion(bf16[11520,256]{1,0:T(8,128)(2,1)} %bitcast.238, bf16[256,512]{1,0:T(8,128)(2,1)S(1)} %copy-done), kind=kOutput, calls=%fused_computation.268 | convolution fusion | flops 3019898880 | bytes 29753344 | tf_op jit(solution)/shard_map/dot_general | solution.py:110
  672.2 6.7 fusion.114
  687.5 25.2 %fusion.21 = bf16[11520,256]{1,0:T(8,128)(2,1)} fusion(bf16[256,512]{1,0:T(8,128)(2,1)S(1)} %copy-done, bf16[11520,256]{1,0:T(8,128)(2,1)} %bitcast.251, f32[11520,512]{1,0:T(8,128)} %fusion.199, bf16[512,256]{1,0:T(8,128)(2,1)S(1)} %copy-done.29), kind=kOutput, calls=%fused_computation.37 | convolution fusion | flops 6166609920 | bytes 35913728 | tf_op jit(solution)/shard_map/dot_general | solution.py:122
  712.7 7.4 fusion.113
  723.7 35.4 %all-to-all-done.6 = bf16[8,48,16,2,128]{4,2,3,1,0:T(8,128)(2,1)} async-done(((bf16[8,48,16,2,128]{4,2,3,1,0:T(8,128)(2,1)}), bf16[8,48,16,2,128]{4,2,3,1,0:T(8,128)(2,1)}, u32[]{:S(2)}, u32[]{:S(2)}) %all-to-all-start.6) | async-done | bytes 3145760 | tf_op jit(solution)/shard_map/all_to_all | solution.py:62
  763.9 15.7 %fusion.24 = bf16[11520,256]{1,0:T(8,128)(2,1)} fusion(bf16[512,256]{1,0:T(8,128)(2,1)S(1)} %copy-done.29, f32[11520,512]{1,0:T(8,128)} %fusion.199, bf16[11520,256]{1,0:T(8,128)(2,1)} %bitcast.239), kind=kOutput, calls=%fused_computation.43 | convolution fusion | flops 3081830400 | bytes 35651584 | tf_op jit(solution)/shard_map/dot_general | solution.py:114
  779.6 5.7 constant_dynamic-slice_fusion.2
  785.3 14.9 %fusion.26 = bf16[11520,256]{1,0:T(8,128)(2,1)} fusion(bf16[512,256]{1,0:T(8,128)(2,1)S(1)} %copy-done.29, f32[11520,512]{1,0:T(8,128)} %fusion.197, bf16[11520,256]{1,0:T(8,128)(2,1)S(1)} %bitcast.237), kind=kOutput, calls=%fused_computation.47 | convolution fusion | flops 3081830400 | bytes 35651584 | tf_op jit(solution)/shard_map/dot_general | solution.py:114
  800.2 7.4 fusion.112
  811.3 23.4 %all-to-all-done.7 = bf16[8,48,16,2,128]{4,2,3,1,0:T(8,128)(2,1)} async-done(((bf16[8,48,16,2,128]{4,2,3,1,0:T(8,128)(2,1)}), bf16[8,48,16,2,128]{4,2,3,1,0:T(8,128)(2,1)}, u32[]{:S(2)}, u32[]{:S(2)}) %all-to-all-start.7) | async-done | bytes 3145760 | tf_op jit(solution)/shard_map/all_to_all | solution.py:62
  839.4 15.7 %fusion.25 = bf16[11520,256]{1,0:T(8,128)(2,1)} fusion(bf16[512,256]{1,0:T(8,128)(2,1)S(1)} %copy-done.29, f32[11520,512]{1,0:T(8,128)} %fusion.198, bf16[11520,256]{1,0:T(8,128)(2,1)} %bitcast.232), kind=kOutput, calls=%fused_computation.45 | convolution fusion | flops 3081830400 | bytes 35651584 | tf_op jit(solution)/shard_map/dot_general | solution.py:114
  855.1 12.4 %fusion.61 = f32[48,384,2,128,1]{3,1,4,2,0:T(8,128)} fusion(bf16[48,384,8,16]{1,0,3,2:T(8,128)(2,1)} %get-tuple-element.26, bf16[8,48,16,2,128]{4,2,3,1,0:T(8,128)(2,1)} %all-to-all-done.6), kind=kOutput, calls=%fused_computation.97 | convolution fusion | flops 1207959552 | bytes 26738688 | tf_op jit(solution)/shard_map/klpr,pkrtc->kltc/dot_general | solution.py:129
  867.5 11.2 %fusion.60 = f32[48,384,2,128,1]{3,1,4,2,0:T(8,128)} fusion(bf16[48,384,8,16]{1,0,3,2:T(8,128)(2,1)S(1)} %bitcast.259, bf16[8,48,16,2,128]{4,2,3,1,0:T(8,128)(2,1)} %all-to-all-done.7), kind=kOutput, calls=%fused_computation.95 | convolution fusion | flops 1207959552 | bytes 26738688 | tf_op jit(solution)/shard_map/klpr,pkrtc->kltc/dot_general | solution.py:129
  878.7 30.8 %all-to-all-done.8 = bf16[8,48,16,2,128]{4,2,3,1,0:T(8,128)(2,1)} async-done(((bf16[8,48,16,2,128]{4,2,3,1,0:T(8,128)(2,1)}), bf16[8,48,16,2,128]{4,2,3,1,0:T(8,128)(2,1)}, u32[]{:S(2)}, u32[]{:S(2)}) %all-to-all-start.8) | async-done | bytes 3145760 | tf_op jit(solution)/shard_map/all_to_all | solution.py:62
  909.5 23.1 %bitcast_add_fusion = f32[48,384,2,128]{3,1,2,0:T(8,128)} fusion(f32[48,384,2,128,1]{3,1,4,2,0:T(8,128)} %fusion.60, f32[48,384,2,128,1]{3,1,4,2,0:T(8,128)} %fusion.61, bf16[48,384,8,16]{1,0,3,2:T(8,128)(2,1)} %get-tuple-element.24, bf16[8,48,16,2,128]{4,2,3,1,0:T(8,128)(2,1)} %all-to-all-done.8), kind=kOutput, calls=%fused_computation.32 | convolution fusion | flops 1217396736 | bytes 64487424 | tf_op jit(solution)/shard_map/klpr,pkrtc->kltc/dot_general | solution.py:129
  932.6 12.8 %add_reduce_fusion.2 = (f32[384,128]{1,0:T(8,128)S(1)}, f32[384,128]{1,0:T(8,128)S(1)}, f32[384,128]{1,0:T(8,128)S(1)}, f32[384,128]{1,0:T(8,128)S(1)}, f32[384,128]{1,0:T(8,128)S(1)}, /*index=5*/f32[384,128]{1,0:T(8,128)S(1)}) fusion(f32[48,384,2,128]{3,1,2,0:T(8,128)} %bitcast_add_fusion, f32[16,384,2,128]{3,1,2,0:T(8,128)} %bitcast_multiply_fusion.2, ...), kind=kLoop, calls=%fused_computation.144 | loop fusion | flops 18579456 | bytes 38928384 | tf_op jit(solution)/shard_map/reduce_sum | solution.py:137
  949.9 15.8 %pad_maximum_fusion = bf16[48,720,256]{2,1,0:T(8,128)(2,1)} fusion(bf16[16,720,256]{2,1,0:T(8,128)(2,1)} %bitcast.249, bf16[16,720,256]{2,1,0:T(8,128)(2,1)} %bitcast.252, bf16[16,720,256]{2,1,0:T(8,128)(2,1)} %bitcast.250), kind=kLoop, calls=%fused_computation.35 | loop fusion | flops 17694720 | bytes 35389440 | tf_op jit(solution)/shard_map/concatenate | solution.py:142
  (159 shorter events, 113.9 us)
Async XLA Ops:
  0.6 579.2 %copy-start = (bf16[256,512]{1,0:T(8,128)(2,1)S(1)}, bf16[256,512]{1,0:T(8,128)(2,1)}, u32[]{:S(2)}) copy-start(bf16[256,512]{1,0:T(8,128)(2,1)} %param.14) | copy-start | bytes 786436
  0.7 12.5 %copy-start.28 = (s32[384]{0:T(512)S(1)}, s32[384]{0:T(512)}, u32[]{:S(2)}) copy-start(s32[384]{0:T(512)} %param.17) | copy-start | bytes 4612
  0.7 12.6 %copy-start.25 = (s32[384]{0:T(512)S(1)}, s32[384]{0:T(512)}, u32[]{:S(2)}) copy-start(s32[384]{0:T(512)} %param.16) | copy-start | bytes 4612
  0.7 12.6 %copy-start.1 = (f32[384]{0:T(512)S(1)}, f32[384]{0:T(512)}, u32[]{:S(2)}) copy-start(f32[384]{0:T(512)} %param.12) | copy-start | bytes 4612
  12.7 14.2 %collective-permute-start = (bf16[48,720,128]{2,1,0:T(8,128)(2,1)}, bf16[48,720,128]{2,1,0:T(8,128)(2,1)}, u32[]{:S(2)}, u32[]{:S(2)}) collective-permute-start(bf16[48,720,128]{2,1,0:T(8,128)(2,1)} %get-tuple-element.23), channel_id=1, source_target_pairs={{0,1},{1,0},{2,3},{3,2},{4,5},{5,4},{6,7},{7,6},{8,9},{9,8},{10,11... | collective-permute-start | bytes 26542088 | tf_op jit(solution)/shard_map/ppermute | solution.py:59
  14.1 21.6 %copy-start.26 = (s32[1440]{0:T(1024)}, s32[1440]{0:T(1024)S(1)}, u32[]{:S(2)}) copy-start(s32[1440]{0:T(1024)S(1)} %add_select_fusion.2) | copy-start | bytes 17284
  24.7 11.1 %copy-start.14 = (bf16[1440,1,8,3,16]{0,4,3,2,1:T(8,128)(2,1)}, bf16[1440,1,8,3,16]{0,4,3,2,1:T(8,128)(2,1)S(1)}, u32[]{:S(2)}) copy-start(bf16[1440,1,8,3,16]{0,4,3,2,1:T(8,128)(2,1)S(1)} %get-tuple-element.66) | copy-start | bytes 3317764
  24.7 11.1 %copy-start.15 = (bf16[1440,1,8,3,16]{0,4,3,2,1:T(8,128)(2,1)}, bf16[1440,1,8,3,16]{0,4,3,2,1:T(8,128)(2,1)S(1)}, u32[]{:S(2)}) copy-start(bf16[1440,1,8,3,16]{0,4,3,2,1:T(8,128)(2,1)S(1)} %get-tuple-element.67) | copy-start | bytes 3317764
  38.2 78.2 %all-to-all-start.1 = ((bf16[8,16,48,2,128]{4,2,3,1,0:T(8,128)(2,1)}), bf16[8,16,48,2,128]{4,2,3,1,0:T(8,128)(2,1)S(1)}, u32[]{:S(2)}, u32[]{:S(2)}) async-start(bf16[8,16,48,2,128]{4,2,3,1,0:T(8,128)(2,1)} %copy.72), calls=%async_computation.1 | async-start | bytes 6291456 | tf_op jit(solution)/shard_map/all_to_all | solution.py:62
  116.4 74.7 %all-to-all-start = ((bf16[8,16,48,2,128]{4,2,3,1,0:T(8,128)(2,1)}), bf16[8,16,48,2,128]{4,2,3,1,0:T(8,128)(2,1)}, u32[]{:S(2)}, u32[]{:S(2)}) async-start(bf16[8,16,48,2,128]{4,2,3,1,0:T(8,128)(2,1)} %copy.68), calls=%async_computation | async-start | bytes 6291456 | tf_op jit(solution)/shard_map/all_to_all | solution.py:62
  191.1 74.8 %all-to-all-start.2 = ((bf16[8,16,48,2,128]{4,2,3,1,0:T(8,128)(2,1)}), bf16[8,16,48,2,128]{4,2,3,1,0:T(8,128)(2,1)}, u32[]{:S(2)}, u32[]{:S(2)}) async-start(bf16[8,16,48,2,128]{4,2,3,1,0:T(8,128)(2,1)} %copy.76), calls=%async_computation.2 | async-start | bytes 6291456 | tf_op jit(solution)/shard_map/all_to_all | solution.py:62
  223.5 11.4 %copy-start.6 = (bf16[48,8,16,384]{3,2,1,0:T(8,128)(2,1)}, bf16[48,8,16,384]{3,2,1,0:T(8,128)(2,1)S(1)}, u32[]{:S(2)}) copy-start(bf16[48,8,16,384]{3,2,1,0:T(8,128)(2,1)S(1)} %copy.137) | copy-start | bytes 14155780
  234.9 36.1 %slice-start.2 = ((s8[6291456]{0:T(1024)(128)(4,1)}), s8[2097152]{0:T(1024)(128)(4,1)S(1)}, s32[]{:S(2)}) async-start(s8[6291456]{0:T(1024)(128)(4,1)} %bitcast.240), calls=%async_computation.12 | async-start | bytes 4194304
  265.9 7.4 copy-start.23
  271.0 7.9 copy-start.5
  298.3 74.6 %all-to-all-start.5 = ((bf16[8,48,16,2,128]{4,2,3,1,0:T(8,128)(2,1)}), bf16[8,48,16,2,128]{4,2,3,1,0:T(8,128)(2,1)}, u32[]{:S(2)}, u32[]{:S(2)}) async-start(bf16[8,48,16,2,128]{4,2,3,1,0:T(8,128)(2,1)} %copy.84), calls=%async_computation.5 | async-start | bytes 6291456 | tf_op jit(solution)/shard_map/all_to_all | solution.py:62
  304.5 72.9 %copy-start.8 = (bf16[8,16,16,2,128]{4,2,0,3,1:T(8,128)(2,1)S(1)}, bf16[8,16,16,2,128]{4,2,0,3,1:T(8,128)(2,1)}, u32[]{:S(2)}) copy-start(bf16[8,16,16,2,128]{4,2,0,3,1:T(8,128)(2,1)} %get-tuple-element.54) | copy-start | bytes 3145732
  372.9 74.6 %all-to-all-start.4 = ((bf16[8,48,16,2,128]{4,2,3,1,0:T(8,128)(2,1)}), bf16[8,48,16,2,128]{4,2,3,1,0:T(8,128)(2,1)}, u32[]{:S(2)}, u32[]{:S(2)}) async-start(bf16[8,48,16,2,128]{4,2,3,1,0:T(8,128)(2,1)} %copy.82), calls=%async_computation.4 | async-start | bytes 6291456 | tf_op jit(solution)/shard_map/all_to_all | solution.py:62
  377.8 74.6 %copy-start.27 = (s32[1440]{0:T(1024)S(1)}, s32[1440]{0:T(1024)}, u32[]{:S(2)}) copy-start(s32[1440]{0:T(1024)} %copy-done.26) | copy-start | bytes 17284
  447.5 75.0 %all-to-all-start.3 = ((bf16[8,48,16,2,128]{4,2,3,1,0:T(8,128)(2,1)}), bf16[8,48,16,2,128]{4,2,3,1,0:T(8,128)(2,1)}, u32[]{:S(2)}, u32[]{:S(2)}) async-start(bf16[8,48,16,2,128]{4,2,3,1,0:T(8,128)(2,1)} %copy.80), calls=%async_computation.3 | async-start | bytes 6291456 | tf_op jit(solution)/shard_map/all_to_all | solution.py:62
  462.9 9.9 %copy-start.16 = (bf16[1440,1,384]{2,0,1:T(8,128)(2,1)}, bf16[1440,1,384]{2,0,1:T(8,128)(2,1)S(1)}, u32[]{:S(2)}) copy-start(bf16[1440,1,384]{2,0,1:T(8,128)(2,1)S(1)} %get-tuple-element.68) | copy-start | bytes 3317764
  462.9 9.9 %copy-start.19 = (bf16[1440,1,384]{2,0,1:T(8,128)(2,1)}, bf16[1440,1,384]{2,0,1:T(8,128)(2,1)S(1)}, u32[]{:S(2)}) copy-start(bf16[1440,1,384]{2,0,1:T(8,128)(2,1)S(1)} %get-tuple-element.69) | copy-start | bytes 3317764
  532.7 23.6 %collective-permute-start.1 = (bf16[16,720,128]{2,1,0:T(8,128)(2,1)}, bf16[16,720,128]{2,1,0:T(8,128)(2,1)}, u32[]{:S(2)}, u32[]{:S(2)}) collective-permute-start(bf16[16,720,128]{2,1,0:T(8,128)(2,1)} %get-tuple-element.43), channel_id=1, source_target_pairs={{0,1},{1,0},{2,3},{3,2},{4,5},{5,4},{6,7},{7,6},{8,9},{9,8},{10,11... | collective-permute-start | bytes 8847368 | tf_op jit(solution)/shard_map/ppermute | solution.py:100
  532.7 23.6 %collective-permute-start.3 = (bf16[16,720,128]{2,1,0:T(8,128)(2,1)}, bf16[16,720,128]{2,1,0:T(8,128)(2,1)}, u32[]{:S(2)}, u32[]{:S(2)}) collective-permute-start(bf16[16,720,128]{2,1,0:T(8,128)(2,1)} %get-tuple-element.47), channel_id=1, source_target_pairs={{0,1},{1,0},{2,3},{3,2},{4,5},{5,4},{6,7},{7,6},{8,9},{9,8},{10,11... | collective-permute-start | bytes 8847368 | tf_op jit(solution)/shard_map/ppermute | solution.py:100
  533.2 23.0 %collective-permute-start.2 = (bf16[16,720,128]{2,1,0:T(8,128)(2,1)}, bf16[16,720,128]{2,1,0:T(8,128)(2,1)}, u32[]{:S(2)}, u32[]{:S(2)}) collective-permute-start(bf16[16,720,128]{2,1,0:T(8,128)(2,1)} %get-tuple-element.45), channel_id=1, source_target_pairs={{0,1},{1,0},{2,3},{3,2},{4,5},{5,4},{6,7},{7,6},{8,9},{9,8},{10,11... | collective-permute-start | bytes 8847368 | tf_op jit(solution)/shard_map/ppermute | solution.py:100
  533.2 16.3 %slice-start.6 = ((s8[17694720]{0:T(1024)(128)(4,1)}), s8[4194304]{0:T(1024)(128)(4,1)S(1)}, s32[]{:S(2)}) async-start(s8[17694720]{0:T(1024)(128)(4,1)} %bitcast.247), calls=%async_computation.16 | async-start | bytes 8388608
  533.2 16.3 %slice-start.7 = ((s8[17694720]{0:T(1024)(128)(4,1)}), s8[4194304]{0:T(1024)(128)(4,1)S(1)}, s32[]{:S(2)}) async-start(s8[17694720]{0:T(1024)(128)(4,1)} %bitcast.247), calls=%async_computation.17 | async-start | bytes 8388608
  533.2 16.3 %slice-start.8 = ((s8[17694720]{0:T(1024)(128)(4,1)}), s8[4194304]{0:T(1024)(128)(4,1)S(1)}, s32[]{:S(2)}) async-start(s8[17694720]{0:T(1024)(128)(4,1)} %bitcast.247), calls=%async_computation.18 | async-start | bytes 8388608
  579.9 9.6 copy-start.3
  579.9 9.6 copy-start.29
  620.2 52.0 %collective-permute-start.4 = (bf16[16,720,128]{2,1,0:T(8,128)(2,1)}, bf16[16,720,128]{2,1,0:T(8,128)(2,1)}, u32[]{:S(2)}, u32[]{:S(2)}) collective-permute-start(bf16[16,720,128]{2,1,0:T(8,128)(2,1)} %get-tuple-element.39), channel_id=1, source_target_pairs={{0,1},{1,0},{2,3},{3,2},{4,5},{5,4},{6,7},{7,6},{8,9},{9,8},{10,11... | collective-permute-start | bytes 8847368 | tf_op jit(solution)/shard_map/ppermute | solution.py:59
  659.7 53.0 %collective-permute-start.5 = (bf16[16,720,128]{2,1,0:T(8,128)(2,1)}, bf16[16,720,128]{2,1,0:T(8,128)(2,1)}, u32[]{:S(2)}, u32[]{:S(2)}) collective-permute-start(bf16[16,720,128]{2,1,0:T(8,128)(2,1)} %get-tuple-element.41), channel_id=1, source_target_pairs={{0,1},{1,0},{2,3},{3,2},{4,5},{5,4},{6,7},{7,6},{8,9},{9,8},{10,11... | collective-permute-start | bytes 8847368 | tf_op jit(solution)/shard_map/ppermute | solution.py:59
  659.8 12.5 %copy-start.9 = (bf16[16,720,128]{2,1,0:T(8,128)(2,1)S(1)}, bf16[16,720,128]{2,1,0:T(8,128)(2,1)}, u32[]{:S(2)}) copy-start(bf16[16,720,128]{2,1,0:T(8,128)(2,1)} %get-tuple-element.38) | copy-start | bytes 8847364
  659.8 12.5 %copy-start.17 = (bf16[1440,1,384]{2,0,1:T(8,128)(2,1)S(1)}, bf16[1440,1,384]{2,0,1:T(8,128)(2,1)}, u32[]{:S(2)}) copy-start(bf16[1440,1,384]{2,0,1:T(8,128)(2,1)} %copy-done.16) | copy-start | bytes 3317764
  659.8 12.5 %copy-start.20 = (bf16[1440,1,384]{2,0,1:T(8,128)(2,1)S(1)}, bf16[1440,1,384]{2,0,1:T(8,128)(2,1)}, u32[]{:S(2)}) copy-start(bf16[1440,1,384]{2,0,1:T(8,128)(2,1)} %copy-done.19) | copy-start | bytes 3317764
  682.7 76.5 %all-to-all-start.6 = ((bf16[8,48,16,2,128]{4,2,3,1,0:T(8,128)(2,1)}), bf16[8,48,16,2,128]{4,2,3,1,0:T(8,128)(2,1)}, u32[]{:S(2)}, u32[]{:S(2)}) async-start(bf16[8,48,16,2,128]{4,2,3,1,0:T(8,128)(2,1)} %copy.87), calls=%async_computation.6 | async-start | bytes 6291456 | tf_op jit(solution)/shard_map/all_to_all | solution.py:62
  759.1 26.1 %slice-start = ((s8[5898240]{0:T(1024)(128)(4,1)}), s8[1703936]{0:T(1024)(128)(4,1)S(1)}, s32[]{:S(2)}) async-start(s8[5898240]{0:T(1024)(128)(4,1)} %bitcast.235), calls=%async_computation.10 | async-start | bytes 3407872
  759.1 75.6 %all-to-all-start.7 = ((bf16[8,48,16,2,128]{4,2,3,1,0:T(8,128)(2,1)}), bf16[8,48,16,2,128]{4,2,3,1,0:T(8,128)(2,1)}, u32[]{:S(2)}, u32[]{:S(2)}) async-start(bf16[8,48,16,2,128]{4,2,3,1,0:T(8,128)(2,1)} %copy.90), calls=%async_computation.7 | async-start | bytes 6291456 | tf_op jit(solution)/shard_map/all_to_all | solution.py:62
  763.9 21.4 %slice-start.1 = ((s8[5898240]{0:T(1024)(128)(4,1)}), s8[4194304]{0:T(1024)(128)(4,1)S(1)}, s32[]{:S(2)}) async-start(s8[5898240]{0:T(1024)(128)(4,1)} %bitcast.235), calls=%async_computation.11 | async-start | bytes 8388608
  785.3 15.0 %copy-start.18 = (bf16[1440,1,384]{2,0,1:T(8,128)(2,1)S(1)}, bf16[1440,1,384]{2,0,1:T(8,128)(2,1)}, u32[]{:S(2)}) copy-start(bf16[1440,1,384]{2,0,1:T(8,128)(2,1)} %copy-done.16) | copy-start | bytes 3317764
  785.3 15.0 %copy-start.21 = (bf16[1440,1,384]{2,0,1:T(8,128)(2,1)S(1)}, bf16[1440,1,384]{2,0,1:T(8,128)(2,1)}, u32[]{:S(2)}) copy-start(bf16[1440,1,384]{2,0,1:T(8,128)(2,1)} %copy-done.19) | copy-start | bytes 3317764
  785.3 15.0 %collective-permute-start.6 = (bf16[16,720,128]{2,1,0:T(8,128)(2,1)}, bf16[16,720,128]{2,1,0:T(8,128)(2,1)}, u32[]{:S(2)}, u32[]{:S(2)}) collective-permute-start(bf16[16,720,128]{2,1,0:T(8,128)(2,1)} %get-tuple-element.37), channel_id=1, source_target_pairs={{0,1},{1,0},{2,3},{3,2},{4,5},{5,4},{6,7},{7,6},{8,9},{9,8},{10,11... | collective-permute-start | bytes 8847368 | tf_op jit(solution)/shard_map/ppermute | solution.py:59
  834.8 32.7 %slice-start.11 = ((s8[4718592]{0:T(1024)(128)(4,1)}), s8[524288]{0:T(1024)(128)(4,1)S(1)}, s32[]{:S(2)}) async-start(s8[4718592]{0:T(1024)(128)(4,1)} %bitcast.258), calls=%async_computation.21 | async-start | bytes 1048576
  834.8 74.8 %all-to-all-start.8 = ((bf16[8,48,16,2,128]{4,2,3,1,0:T(8,128)(2,1)}), bf16[8,48,16,2,128]{4,2,3,1,0:T(8,128)(2,1)}, u32[]{:S(2)}, u32[]{:S(2)}) async-start(bf16[8,48,16,2,128]{4,2,3,1,0:T(8,128)(2,1)} %copy.93), calls=%async_computation.8 | async-start | bytes 6291456 | tf_op jit(solution)/shard_map/all_to_all | solution.py:62
  839.4 28.1 %slice-start.12 = ((s8[4718592]{0:T(1024)(128)(4,1)}), s8[4194304]{0:T(1024)(128)(4,1)S(1)}, s32[]{:S(2)}) async-start(s8[4718592]{0:T(1024)(128)(4,1)} %bitcast.258), calls=%async_computation.22 | async-start | bytes 8388608
  867.5 65.1 %slice-start.4 = ((s8[6291456]{0:T(1024)(128)(4,1)}), s8[2097152]{0:T(1024)(128)(4,1)S(1)}, s32[]{:S(2)}) async-start(s8[6291456]{0:T(1024)(128)(4,1)} %bitcast.242), calls=%async_computation.14 | async-start | bytes 4194304
  909.5 23.1 %slice-start.5 = ((s8[6291456]{0:T(1024)(128)(4,1)}), s8[4194304]{0:T(1024)(128)(4,1)S(1)}, s32[]{:S(2)}) async-start(s8[6291456]{0:T(1024)(128)(4,1)} %bitcast.242), calls=%async_computation.15 | async-start | bytes 8388608
  946.2 19.5 %all-to-all-start.9 = ((f32[8,48,2,128]{3,1,2,0:T(8,128)}), f32[8,48,2,128]{3,1,2,0:T(8,128)S(1)}, u32[]{:S(2)}, u32[]{:S(2)}) async-start(f32[8,48,2,128]{3,1,2,0:T(8,128)} %pad_maximum_fusion.6), calls=%async_computation.9 | async-start | bytes 786432 | tf_op jit(solution)/shard_map/all_to_all | solution.py:62
  (14 other events, 78.3 us)

commit v2 on v1

v2 whole, which is shorter than its diff:
```python
from functools import partial
import math

import jax
import jax.numpy as jnp
from jax import lax
from jax.experimental import pallas as pl
from jax.experimental.pallas import tpu as pltpu
from jax.sharding import PartitionSpec as P


def wave_table(m_order, lon_index, lon_count):
    phase_int = lon_index[:, None] * m_order[None, :] % lon_count
    angle_rad = phase_int.astype(jnp.float32) * (2.0 * math.pi / lon_count)
    norm_scale = 1.0 / math.sqrt(lon_count)
    return jnp.stack(
        [jnp.cos(angle_rad) * norm_scale, -jnp.sin(angle_rad) * norm_scale], axis=1
    ).astype(jnp.bfloat16)


def rotate(coeffs, gains):
    real_part = coeffs[:, 0] * gains[None, 0] - coeffs[:, 1] * gains[None, 1]
    imag_part = coeffs[:, 0] * gains[None, 1] + coeffs[:, 1] * gains[None, 0]
    return jnp.stack([real_part, imag_part], axis=1)


GELU_SCALE = math.sqrt(2.0 / math.pi)
GELU_CUBIC = 0.044715


def mlp_body(
    pieces, az_ref, state_ref, own_ref, came_ref, cot_ref, w_in_ref, w_out_ref, w_out_t_ref,
    w_in_t_ref, *rest
):
    out_ref, d_own_ref, d_other_ref = rest[-3:]
    first = az_ref[0] == 0
    width = own_ref.shape[-1]
    step = state_ref.shape[1] // pieces
    for p in range(pieces):
        at = slice(p * step, (p + 1) * step)
        own = own_ref[0, at].astype(jnp.float32)
        came = came_ref[0, at].astype(jnp.float32)
        spectral = jnp.concatenate(
            [jnp.where(first, own, came), jnp.where(first, came, own)], axis=1
        )
        mixed = (state_ref[0, at].astype(jnp.float32) + spectral).astype(jnp.bfloat16)
        cot = cot_ref[0, at]
        x = jnp.dot(mixed, w_in_ref[...], preferred_element_type=jnp.float32)
        d_hidden = jnp.dot(cot, w_out_t_ref[...], preferred_element_type=jnp.float32)
        square = x * x
        t = jnp.tanh(x * (GELU_SCALE + (GELU_SCALE * GELU_CUBIC) * square))
        half = 0.5 * x
        hidden = (half + half * t).astype(jnp.bfloat16)
        slope = GELU_SCALE + (3.0 * GELU_SCALE * GELU_CUBIC) * square
        rise = 0.5 + 0.5 * t + half * (1.0 - t * t) * slope
        d_pre = (d_hidden * rise).astype(jnp.bfloat16)
        out_ref[0, at] = (
            mixed.astype(jnp.float32)
            + jnp.dot(hidden, w_out_ref[...], preferred_element_type=jnp.float32)
        ).astype(jnp.bfloat16)
        d_mixed = cot.astype(jnp.float32) + jnp.dot(
            d_pre, w_in_t_ref[...], preferred_element_type=jnp.float32
        )
        low, high = d_mixed[:, :width], d_mixed[:, width:]
        d_own_ref[0, at] = jnp.where(first, low, high).astype(jnp.bfloat16)
        d_other_ref[0, at] = jnp.where(first, high, low).astype(jnp.bfloat16)


def mlp(start, az_index, state_grid, spectral, came, cotangent, w_in, w_out, block_out):
    rows, half_lon, channels = state_grid.shape
    rg, _, width = came.shape
    hid = w_in.shape[1]
    pieces = 3 if half_lon % 48 == 0 else 1
    field = pl.BlockSpec((1, half_lon, channels), lambda i: (start + i, 0, 0))
    part = pl.BlockSpec((1, half_lon, width), lambda i: (i, 0, 0))
    whole = lambda a: pl.BlockSpec(a.shape, lambda i: (0, 0))
    w_out_t, w_in_t = w_out.T, w_in.T
    operands = [az_index.reshape(1), state_grid, spectral, came, cotangent, w_in, w_out, w_out_t, w_in_t]
    in_specs = [
        pl.BlockSpec(memory_space=pltpu.SMEM), field, part, part, field,
        whole(w_in), whole(w_out), whole(w_out_t), whole(w_in_t),
    ]
    aliases = {}
    if block_out is not None:
        aliases = {len(operands): 0}
        operands.append(block_out)
        in_specs.append(pl.BlockSpec(memory_space=pl.ANY))
    half = jax.ShapeDtypeStruct((rg, half_lon, width), jnp.bfloat16)
    tokens = rg * half_lon
    return pl.pallas_call(
        partial(mlp_body, pieces),
        grid=(rg,),
        in_specs=in_specs,
        out_specs=[field, part, part],
        out_shape=[jax.ShapeDtypeStruct(state_grid.shape, jnp.bfloat16), half, half],
        input_output_aliases=aliases,
        compiler_params=pltpu.CompilerParams(vmem_limit_bytes=48 * 1024 * 1024),
        cost_estimate=pl.CostEstimate(
            flops=8 * tokens * channels * hid,
            bytes_accessed=10 * tokens * channels,
            transcendentals=tokens * hid,
        ),
    )(*operands)


def gather_body(table_ref, modes_ref, coeffs_ref, out_ref):
    @pl.when(pl.program_id(0) == 0)
    def _():
        out_ref[...] = jnp.zeros_like(out_ref)

    real, imag = out_ref[0], out_ref[1]
    for j in range(table_ref.shape[0]):
        both = jnp.concatenate([modes_ref[:, j, 0], modes_ref[:, j, 1]], axis=2)
        both = both.reshape(both.shape[0] * both.shape[1], both.shape[2])
        d_filt = jnp.dot(table_ref[j], both, preferred_element_type=jnp.float32)
        width = d_filt.shape[1] // 2
        d0, d1 = d_filt[:, :width], d_filt[:, width:]
        c0, c1 = coeffs_ref[j, 0], coeffs_ref[j, 1]
        real += d0 * c0 + d1 * c1
        imag += d1 * c0 - d0 * c1
    out_ref[0] = real
    out_ref[1] = imag


def filter_terms(table_h, d_waves, coeffs):
    waves, degrees, lats = table_h.shape
    shards, _, _, rg, width = d_waves.shape
    if rg % 16 != 0:
        part = table_h.reshape(waves, degrees, shards, rg)
        d = jnp.einsum("klpr,pktrc->ktlc", part, d_waves, preferred_element_type=jnp.float32)
        real = jnp.sum(d[:, 0] * coeffs[:, 0] + d[:, 1] * coeffs[:, 1], axis=0)
        imag = jnp.sum(d[:, 1] * coeffs[:, 0] - d[:, 0] * coeffs[:, 1], axis=0)
        return jnp.stack([real, imag], axis=0)
    kb = 4 if waves % 4 == 0 else 1
    return pl.pallas_call(
        gather_body,
        grid=(waves // kb,),
        in_specs=[
            pl.BlockSpec((kb, degrees, lats), lambda i: (i, 0, 0)),
            pl.BlockSpec((shards, kb, 2, rg, width), lambda i: (0, i, 0, 0, 0)),
            pl.BlockSpec((kb, 2, degrees, width), lambda i: (i, 0, 0, 0)),
        ],
        out_specs=pl.BlockSpec((2, degrees, width), lambda i: (0, 0, 0)),
        out_shape=jax.ShapeDtypeStruct((2, degrees, width), jnp.float32),
        compiler_params=pltpu.CompilerParams(vmem_limit_bytes=48 * 1024 * 1024),
        cost_estimate=pl.CostEstimate(
            flops=4 * waves * degrees * lats * width,
            bytes_accessed=waves * degrees * (2 * lats + 8 * width),
            transcendentals=0,
        ),
    )(table_h, d_waves, coeffs)


def local(
    state_grid, cotangent, legendre, quad_weight, spec_weight, w_in, w_out, lat_order, m_order
):
    polar_count = lax.axis_size("polar")
    az_count = lax.axis_size("azimuth")
    az_index = lax.axis_index("azimuth")
    polar_index = lax.axis_index("polar")
    rows, half_lon, channels = state_grid.shape
    full_lon = half_lon * az_count
    waves = legendre.shape[0]
    degrees = legendre.shape[1]
    row_start = polar_index * rows
    width = channels // az_count
    row_chunks = 3 if rows % 3 == 0 else 1
    rg = rows // row_chunks
    edge = waves // 4
    wave_spans = [slice(0, edge), slice(edge, waves - edge), slice(waves - edge, waves)]
    spans = [slice(h * rg, (h + 1) * rg) for h in range(row_chunks)]
    swap = [(0, 1), (1, 0)]
    gain_local = lax.dynamic_slice_in_dim(spec_weight, az_index * width, width, 2).transpose(1, 0, 2)
    lon_index = (jnp.arange(full_lon, dtype=jnp.int32) + az_index * half_lon) % full_lon
    basis = wave_table(m_order, lon_index, full_lon)
    row_lats = lax.dynamic_slice_in_dim(lat_order, row_start, rows, 0)
    row_quad = jnp.take(quad_weight, row_lats)
    waves_here = lax.dynamic_slice_in_dim(m_order, polar_index * waves, waves, 0)
    lat_pick = (jnp.arange(lat_order.shape[0], dtype=jnp.int32)[:, None] == lat_order[None, :]).astype(
        jnp.bfloat16
    )
    lower_mask = (jnp.arange(degrees, dtype=jnp.int32)[None, :] >= waves_here[:, None]).astype(
        jnp.float32
    )

    def join(own, other):
        return jnp.concatenate([own, lax.ppermute(other, "azimuth", swap)], axis=1)

    def exchange(x):
        return lax.all_to_all(x, "polar", split_axis=0, concat_axis=0, tiled=True)

    lon_full = join(
        lax.dynamic_slice_in_dim(state_grid, az_index * width, width, 2),
        lax.dynamic_slice_in_dim(state_grid, (1 - az_index) * width, width, 2),
    )
    basis_parts = basis.reshape(full_lon, 2, polar_count, waves)
    flat_legendre = legendre.reshape(waves * degrees, -1)

    def pick(columns):
        return jnp.dot(flat_legendre, columns, preferred_element_type=jnp.float32).astype(
            jnp.bfloat16
        )

    table = pick(lat_pick).reshape(waves, degrees, polar_count, rows)
    by_row = lat_pick.reshape(-1, polar_count, rows)
    table_rows = [
        pick(by_row[:, :, span].reshape(-1, polar_count * rg)).reshape(waves, degrees, -1)
        for span in spans
    ]
    tie = lax.optimization_barrier

    arrivals = []
    for ks in wave_spans:
        fourier = jnp.einsum(
            "rnc,ntpk->pktrc", lon_full, basis_parts[..., ks], preferred_element_type=jnp.float32
        )
        weighted = (fourier * row_quad[None, None, None, :, None]).astype(jnp.bfloat16)
        arrivals.append(exchange(weighted))

    coeffs, modes = [], []
    for g, ks in enumerate(wave_spans):
        at_waves = arrivals[g]
        if g == len(wave_spans) - 1:
            at_waves, *modes = tie((at_waves, *modes))
        part = table[ks]
        coeffs_g = jnp.einsum(
            "klpr,pktrc->ktlc", part, at_waves, preferred_element_type=jnp.float32
        ) * lower_mask[ks][:, None, :, None]
        filtered = rotate(coeffs_g, gain_local).astype(jnp.bfloat16)
        modes_g = jnp.einsum(
            "klpr,ktlc->pktrc", part, filtered, preferred_element_type=jnp.float32
        ).astype(jnp.bfloat16)
        coeffs.append(coeffs_g)
        modes.append(modes_g)

    block_out = None

    def middle(h, at_rows, block_out):
        at_rows = at_rows.reshape(polar_count * waves, 2, rg, width)
        spectral = jnp.einsum(
            "ktrc,ntk->rnc", at_rows, basis, preferred_element_type=jnp.float32
        ).astype(jnp.bfloat16)
        came = lax.ppermute(spectral[:, half_lon:], "azimuth", swap)
        block_out, d_own, d_other = mlp(
            h * rg, az_index, state_grid, spectral, came, cotangent, w_in, w_out, block_out
        )
        d_modes = jnp.einsum(
            "rnc,ntk->ktrc", join(d_own, d_other), basis, preferred_element_type=jnp.float32
        ).astype(jnp.bfloat16)
        return d_modes.reshape(polar_count, waves, 2, rg, width), block_out

    outgoing = [jnp.concatenate([m[:, :, :, span] for m in modes], axis=1) for span in spans]
    all_coeffs = jnp.concatenate(coeffs, axis=0)
    if row_chunks == 3:
        at_0, at_1 = exchange(outgoing[0]), exchange(outgoing[1])
        at_0, all_coeffs = tie((at_0, all_coeffs))
        send_0, block_out = middle(0, at_0, None)
        out_2, send_0 = tie((outgoing[2], send_0))
        at_2 = exchange(out_2)
        send_1, block_out = middle(1, at_1, block_out)
        send_0, send_1 = tie((send_0, send_1))
        d_at_0 = exchange(send_0)
        send_2, block_out = middle(2, at_2, block_out)
        send_1, send_2 = tie((send_1, send_2))
        d_at_1 = exchange(send_1)
        d_at_2 = exchange(send_2)
        early = filter_terms(table_rows[0], d_at_0, all_coeffs) + filter_terms(
            table_rows[1], d_at_1, all_coeffs
        )
        d_at_2, early = tie((d_at_2, early))
        terms = early + filter_terms(table_rows[2], d_at_2, all_coeffs)
    else:
        terms = 0.0
        for h in range(row_chunks):
            send, block_out = middle(h, exchange(outgoing[h]), block_out)
            terms += filter_terms(table_rows[h], exchange(send), all_coeffs)

    shares = exchange(
        terms.reshape(2, polar_count, degrees // polar_count, width).transpose(1, 0, 2, 3)
    )
    return (block_out, jnp.sum(shares, axis=0).transpose(1, 0, 2))


def solution(mesh):
    return jax.shard_map(
        local,
        mesh=mesh,
        in_specs=(
            P(("group", "polar"), "azimuth", None),
            P(("group", "polar"), "azimuth", None),
            P("polar", None, None),
            P(),
            P(),
            P(),
            P(),
            P(),
            P(),
        ),
        out_specs=(P(("group", "polar"), "azimuth", None), P("polar", None, ("group", "azimuth"))),
        check_vma=False,
    )
```

time: 976 us -> 817 us (0.84)
  waiting for transfers between devices: 408 us -> 230 us
  matrix products: 319 us -> 158 us
  Pallas kernels: 0 us -> 124 us
  blocking collectives: 0 us -> 90.9 us
  other arithmetic: 82.3 us -> 51.7 us
  starting transfers between devices: 49.3 us -> 39.2 us
    all_to_all x10 -> x8, waiting for transfers between devices: 406 us -> 212 us  [exchange(): return lax.all_to_all(x, 'polar', split_axis=0, concat_axis=0, tiled=True)]
    dot_general x28 -> x19, matrix products: 319 us -> 158 us  [the longest x4 56.5 us: pick(): jnp.dot(flat_legendre, columns, preferred_element_type=jnp.float32)]
    pallas_call x0 -> x6, Pallas kernels: none -> 124 us  [the longest x3 85.2 us: mlp(): pl.pallas_call(partial(mlp_body, pieces), grid=(rg,), in_specs=in_specs,...]
    all_to_all x0 -> x2, blocking collectives: none -> 90.9 us  [exchange(): return lax.all_to_all(x, 'polar', split_axis=0, concat_axis=0, tiled=True)]
    convert_element_type x3 -> x9, local copies, waits for them, and re-layouts: 7.46 us -> 38.1 us  [the longest x3 19.8 us: pick(): jnp.dot(flat_legendre, columns, preferred_element_type=jnp.float32)]
    convert_element_type x1 -> x0, other arithmetic: 23.6 us -> none  [local(): (state_grid[span].astype(jnp.float32) + returned.astype(jnp.float32)).ast...]
    ppermute x7, waiting for transfers between devices: 2.21 us -> 18.3 us  [the longest x4 13 us: join(): return jnp.concatenate([own, lax.ppermute(other, 'azimuth', swap)], axis=1)]
    dynamic_slice x4 -> x1, local copies, waits for them, and re-layouts: 28.1 us -> 12 us  [local(): lax.dynamic_slice_in_dim(state_grid, az_index * width, width, 2)]
  transfers between devices with their start and end apart: 17 -> 15, of which waited for: 10 -> 11; matrix products, arithmetic and copies ran while one was open for 35% -> 32% of each run, Pallas kernels for 0% -> 14%
where the time goes in v2:
time: 817 us; the launch traced here: 808 us
  waiting for transfers between devices  230 us (28%)
  matrix products  158 us (19%)
  Pallas kernels  124 us (15%)
  local copies, waits for them, and re-layouts  112 us (14%)
  blocking collectives  90.9 us (11%)
  other arithmetic  51.7 us (6%)
  starting transfers between devices  39.2 us (5%)
    all_to_all x8, waiting for transfers between devices, exchange(): return lax.all_to_all(x, 'polar', split_axis=0, concat_axis=0, tiled=True)  212 us
    all_to_all x2, blocking collectives, exchange(): return lax.all_to_all(x, 'polar', split_axis=0, concat_axis=0, tiled=True)  90.9 us
    pallas_call x3, Pallas kernels, mlp(): pl.pallas_call(partial(mlp_body, pieces), grid=(rg,), in_specs=in_specs,...  85.2 us
    dot_general x4, matrix products, pick(): jnp.dot(flat_legendre, columns, preferred_element_type=jnp.float32)  56.5 us
    pallas_call x3, Pallas kernels, filter_terms(): pl.pallas_call(gather_body, grid=(waves // kb,), in_specs=[pl.BlockSpec((...  39.2 us
    all_to_all x8, starting transfers between devices, exchange(): return lax.all_to_all(x, 'polar', split_axis=0, concat_axis=0, tiled=True)  38.5 us
    dot_general x3, matrix products, local(): jnp.einsum('rnc,ntpk->pktrc', lon_full, basis_parts[..., ks], preferred_e...  29.7 us
    another operation x5, other arithmetic  26.8 us
  transfers between devices with their start and end apart: 15, of which 11 were waited for; matrix products, arithmetic and copies ran while one was open for 32% of the time, Pallas kernels for 14%

profile of v2, /device:TPU:0, one launch (start us, length us, event | category | flops | bytes accessed | tf_op | source)
XLA Modules:
  0.0 808.0 jit_solution(10018804149579871880)
XLA Ops:
  0.7 12.0 %constant_dynamic-slice_fusion.1 = (bf16[48,720,128]{2,1,0:T(8,128)(2,1)}, bf16[48,720,128]{2,1,0:T(8,128)(2,1)}) fusion(bf16[48,720,256]{2,1,0:T(8,128)(2,1)} %state_ref.5, s32[]{:T(128)S(6)} %select_n.63, s32[]{:T(128)S(6)} %select_n.64), kind=kLoop, calls=%fused_computation.142 | loop fusion | bytes 35389448 | tf_op jit(solution)/shard_map/dynamic_slice | solution.py:193
  14.2 10.4 %multiply_convert_fusion.3 = (bf16[1440,1,8,48]{0,3,2,1:T(8,128)(2,1)S(1)}, bf16[1440,1,8,48]{0,3,2,1:T(8,128)(2,1)S(1)}) fusion(s32[8,48]{1,0:T(8,128)S(1)} %mul.280, s32[1440]{0:T(1024)S(1)} %add_select_fusion.2), kind=kLoop, calls=%fused_computation.95 | loop fusion | flops 7741440 | bytes 2219136 | tf_op jit(solution)/shard_map/convert.7
  26.9 8.9 %fusion.44 = bf16[8,12,2,48,128]{4,1,3,0,2:T(8,128)(2,1)S(1)} fusion(f32[48]{0:T(128)S(1)} %and_select_fusion, bf16[48,720,128]{2,1,0:T(8,128)(2,1)} %collective-permute-done, bf16[48,720,128]{2,1,0:T(8,128)(2,1)} %get-tuple-element.48, bf16[1440,1,8,48]{0,3,2,1:T(8,128)(2,1)S(1)} %get-tuple-element.75, bf16[1440,1,8,48]{0,3,2,1:T(8,128)(2,1)S(1)} %get-tuple-element.74), kind=kOutput, calls=%fused_computation.65 | convolution fusion | flops 3436240896 | bytes 22266048 | tf_op jit(solution)/shard_map/rnc,ntpk->pktrc/dot_general | solution.py:214
  37.8 7.2 all-to-all-start.1
  45.0 11.7 %fusion.21 = bf16[8,24,2,48,128]{4,1,3,0,2:T(8,128)(2,1)S(1)} fusion(f32[48]{0:T(128)S(1)} %and_select_fusion, bf16[48,720,128]{2,1,0:T(8,128)(2,1)} %collective-permute-done, bf16[48,720,128]{2,1,0:T(8,128)(2,1)} %get-tuple-element.48, bf16[1440,1,8,48]{0,3,2,1:T(8,128)(2,1)} %copy-done.24, bf16[1440,1,8,48]{0,3,2,1:T(8,128)(2,1)} %copy-done.25), kind=kOutput, calls=%fused_computation.38 | convolution fusion | flops 6837092352 | bytes 24625344 | tf_op jit(solution)/shard_map/rnc,ntpk->pktrc/dot_general | solution.py:214
  59.8 39.4 %all-to-all-done.1 = bf16[8,12,2,48,128]{4,3,2,1,0:T(8,128)(2,1)S(1)} async-done(((bf16[8,12,2,48,128]{4,3,2,1,0:T(8,128)(2,1)}), bf16[8,12,2,48,128]{4,3,2,1,0:T(8,128)(2,1)S(1)}, u32[]{:S(2)}, u32[]{:S(2)}) %all-to-all-start.1) | async-done | bytes 2359328 | tf_op jit(solution)/shard_map/all_to_all | solution.py:190
  99.2 4.8 all-to-all-start.2
  104.0 20.9 %fusion = bf16[18432,384]{0,1:T(8,128)(2,1)} fusion(bf16[18432,384]{1,0:T(8,128)(2,1)} %bitcast.192, s32[384]{0:T(512)S(1)} %copy-done.33), kind=kOutput, calls=%fused_computation.2 | convolution fusion | flops 5443190784 | bytes 28313088 | tf_op jit(solution)/shard_map/dot_general | solution.py:200
  133.2 6.4 fusion.111
  139.6 7.2 slice.124
  146.9 7.2 slice.139
  155.2 9.2 %fusion.43 = bf16[8,12,2,48,128]{4,1,3,0,2:T(8,128)(2,1)S(1)} fusion(f32[48]{0:T(128)S(1)} %and_select_fusion, bf16[48,720,128]{2,1,0:T(8,128)(2,1)} %collective-permute-done, bf16[48,720,128]{2,1,0:T(8,128)(2,1)} %get-tuple-element.48, bf16[1440,1,8,48]{0,3,2,1:T(8,128)(2,1)} %copy-done.25, bf16[1440,1,8,48]{0,3,2,1:T(8,128)(2,1)} %copy-done.24), kind=kOutput, calls=%fused_computation.64 | convolution fusion | flops 3436240896 | bytes 22266048 | tf_op jit(solution)/shard_map/rnc,ntpk->pktrc/dot_general | solution.py:214
  170.3 37.5 %all-to-all-done.2 = bf16[8,24,2,48,128]{4,3,2,1,0:T(8,128)(2,1)} async-done(((bf16[8,24,2,48,128]{4,3,2,1,0:T(8,128)(2,1)}), bf16[8,24,2,48,128]{4,3,2,1,0:T(8,128)(2,1)}, u32[]{:S(2)}, u32[]{:S(2)}) %all-to-all-start.2) | async-done | bytes 4718624 | tf_op jit(solution)/shard_map/all_to_all | solution.py:190
  219.8 11.0 %fusion.38 = f32[24,2,128,384]{2,3,0,1:T(8,128)} fusion(bf16[24,384,8,48,1]{1,0,3,2,4:T(8,128)(2,1)} %bitcast.197, bf16[8,24,2,48,128]{4,3,2,1,0:T(8,128)(2,1)} %all-to-all-done.2), kind=kOutput, calls=%fused_computation.62 | convolution fusion | flops 1811939328 | bytes 21233664 | tf_op jit(solution)/shard_map/klpr,pktrc->ktlc/dot_general | solution.py:226
  230.8 5.0 fusion.4
  240.9 9.2 %convert_bitcast_fusion = bf16[8,24,2,48,128]{4,3,0,2,1:T(8,128)(2,1)} fusion(bf16[24,384,8,48,1]{1,0,3,2,4:T(8,128)(2,1)} %bitcast.198, bf16[24,1,384,128]{3,2,1,0:T(8,128)(2,1)} %get-tuple-element.53, bf16[24,1,384,128]{3,2,1,0:T(8,128)(2,1)} %get-tuple-element.52), kind=kOutput, calls=%fused_computation.47 | convolution fusion | flops 1823735808 | bytes 16515072 | tf_op jit(solution)/shard_map/klpr,ktlc->pktrc/dot_general | solution.py:230
  250.1 15.7 %all-to-all-done = bf16[8,12,2,48,128]{4,3,2,1,0:T(8,128)(2,1)S(1)} async-done(((bf16[8,12,2,48,128]{4,3,2,1,0:T(8,128)(2,1)}), bf16[8,12,2,48,128]{4,3,2,1,0:T(8,128)(2,1)S(1)}, u32[]{:S(2)}, u32[]{:S(2)}) %all-to-all-start) | async-done | bytes 2359328 | tf_op jit(solution)/shard_map/all_to_all | solution.py:190
  282.5 4.7 all-to-all-start.3
  287.1 11.2 %multiply_convert_fusion.6 = (bf16[1440,1,384]{2,0,1:T(8,128)(2,1)}, bf16[1440,1,384]{2,0,1:T(8,128)(2,1)}) fusion(s32[384]{0:T(512)S(1)} %copy-done.37, s32[1440]{0:T(1024)S(1)} %add_select_fusion.2), kind=kLoop, calls=%fused_computation.113 | loop fusion | flops 7741440 | bytes 2219136 | tf_op jit(solution)/shard_map/convert.8
  298.4 14.6 %pad_maximum_fusion.coeffs_ref = f32[48,2,384,128]{3,2,1,0:T(8,128)} fusion(f32[12,2,384,128]{3,2,1,0:T(8,128)} %copy-done.15, f32[24,2,384,128]{3,2,1,0:T(8,128)} %copy-done.13, f32[12,2,384,128]{3,2,1,0:T(8,128)} %copy-done.14), kind=kLoop, calls=%fused_computation.9 | loop fusion | flops 9437184 | bytes 37748736 | tf_op jit(solution)/shard_map/concatenate | solution.py:253
  312.9 44.4 %all-to-all-done.3 = bf16[8,48,2,16,128]{4,3,2,1,0:T(8,128)(2,1)} async-done(((bf16[8,48,2,16,128]{4,3,2,1,0:T(8,128)(2,1)}), bf16[8,48,2,16,128]{4,3,2,1,0:T(8,128)(2,1)}, u32[]{:S(2)}, u32[]{:S(2)}) %all-to-all-start.3) | async-done | bytes 3145760 | tf_op jit(solution)/shard_map/all_to_all | solution.py:190
  357.3 7.2 fusion.27.own_ref
  375.5 28.1 %shard_map.104 = (bf16[48,720,256]{2,1,0:T(8,128)(2,1)}, bf16[16,720,128]{2,1,0:T(8,128)(2,1)S(1)}, bf16[16,720,128]{2,1,0:T(8,128)(2,1)}) custom-call(s32[1]{0:T(128)} %bitcast.az_ref, bf16[48,720,256]{2,1,0:T(8,128)(2,1)} %state_ref.5, bf16[16,1440,128]{2,1,0:T(8,128)(2,1)} %copy-done.16, bf16[16,720,128]{2,1,0:T(8,128)(2,1)} %collective-permute-done.1.came_ref, ...), custom_call_target="tpu_custom_call" | custom-call | flops 12079595520 | bytes 29491200 | tf_op jit(solution)/shard_map/pallas_call | solution.py:90
  404.0 5.1 collective-permute-done.2
  409.1 5.4 convert_bitcast_fusion.3
  420.4 24.8 %all-to-all-done.5 = bf16[8,48,2,16,128]{4,3,2,1,0:T(8,128)(2,1)} async-done(((bf16[8,48,2,16,128]{4,3,2,1,0:T(8,128)(2,1)}), bf16[8,48,2,16,128]{4,3,2,1,0:T(8,128)(2,1)}, u32[]{:S(2)}, u32[]{:S(2)}) %all-to-all-start.5) | async-done | bytes 3145760 | tf_op jit(solution)/shard_map/all_to_all | solution.py:190
  445.3 4.9 all-to-all-start.4
  450.2 7.1 fusion.29.own_ref
  457.6 5.4 collective-permute-done.4.came_ref
  464.5 28.2 %shard_map.105 = (bf16[48,720,256]{2,1,0:T(8,128)(2,1)}, bf16[16,720,128]{2,1,0:T(8,128)(2,1)S(1)}, bf16[16,720,128]{2,1,0:T(8,128)(2,1)}) custom-call(s32[1]{0:T(128)} %bitcast.az_ref, bf16[48,720,256]{2,1,0:T(8,128)(2,1)} %state_ref.5, bf16[16,1440,128]{2,1,0:T(8,128)(2,1)} %copy-done.18, ...), custom_call_target="tpu_custom_call", output_to_operand_aliasing={{0}: (9, {})} | custom-call | flops 12079595520 | bytes 29491200 | tf_op jit(solution)/shard_map/pallas_call | solution.py:90
  494.5 25.8 %all-to-all-done.4 = bf16[8,48,2,16,128]{4,3,2,1,0:T(8,128)(2,1)} async-done(((bf16[8,48,2,16,128]{4,3,2,1,0:T(8,128)(2,1)}), bf16[8,48,2,16,128]{4,3,2,1,0:T(8,128)(2,1)}, u32[]{:S(2)}, u32[]{:S(2)}) %all-to-all-start.4) | async-done | bytes 3145760 | tf_op jit(solution)/shard_map/all_to_all | solution.py:190
  520.3 7.1 fusion.28.own_ref
  531.4 6.7 convert_bitcast_fusion.2
  548.5 28.9 %shard_map.106 = (bf16[48,720,256]{2,1,0:T(8,128)(2,1)}, bf16[16,720,128]{2,1,0:T(8,128)(2,1)S(1)}, bf16[16,720,128]{2,1,0:T(8,128)(2,1)}) custom-call(s32[1]{0:T(128)} %bitcast.az_ref, bf16[48,720,256]{2,1,0:T(8,128)(2,1)} %state_ref.5, bf16[16,1440,128]{2,1,0:T(8,128)(2,1)} %copy-done.17, ...), custom_call_target="tpu_custom_call", output_to_operand_aliasing={{0}: (9, {})} | custom-call | flops 12079595520 | bytes 29491200 | tf_op jit(solution)/shard_map/pallas_call | solution.py:90
  577.4 5.6 collective-permute-done.6
  583.0 5.4 convert_bitcast_fusion.1
  592.1 24.4 %all-to-all-done.7.modes_ref = bf16[8,48,2,16,128]{4,3,2,1,0:T(8,128)(2,1)S(1)} async-done(((bf16[8,48,2,16,128]{4,3,2,1,0:T(8,128)(2,1)}), bf16[8,48,2,16,128]{4,3,2,1,0:T(8,128)(2,1)S(1)}, u32[]{:S(2)}, u32[]{:S(2)}) %all-to-all-start.7) | async-done | bytes 3145760 | tf_op jit(solution)/shard_map/all_to_all | solution.py:190
  616.5 74.8 %all_to_all.50.modes_ref = bf16[8,48,2,16,128]{4,3,2,1,0:T(8,128)(2,1)} all-to-all(bf16[8,48,2,16,128]{4,3,2,1,0:T(8,128)(2,1)} %bitcast.214), channel_id=1, replica_groups=mesh['group'=2,'polar'=8,'azimuth'=2] {'polar'}, dimensions={0} | all-to-all | bytes 6291456 | tf_op jit(solution)/shard_map/all_to_all | solution.py:190
  696.1 11.9 %fusion.2 = bf16[18432,128]{0,1:T(8,128)(2,1)} fusion(pred[384,128]{0,1:T(8,128)(4,1)S(1)} %bitcast.227, bf16[18432,384]{1,0:T(8,128)(2,1)} %bitcast.193), kind=kOutput, calls=%fused_computation.7 | convolution fusion | flops 1814298624 | bytes 18923520 | tf_op jit(solution)/shard_map/dot_general | solution.py:200
  708.0 6.6 copy.84
  714.6 11.9 %fusion.1 = bf16[18432,128]{0,1:T(8,128)(2,1)} fusion(pred[384,128]{0,1:T(8,128)(4,1)S(1)} %bitcast.226, bf16[18432,384]{1,0:T(8,128)(2,1)} %bitcast.194), kind=kOutput, calls=%fused_computation.6 | convolution fusion | flops 1814298624 | bytes 18923520 | tf_op jit(solution)/shard_map/dot_general | solution.py:200
  726.5 6.6 copy.83
  733.1 11.9 %fusion.3 = bf16[18432,128]{0,1:T(8,128)(2,1)} fusion(pred[384,128]{0,1:T(8,128)(4,1)S(1)} %bitcast.225, bf16[18432,384]{1,0:T(8,128)(2,1)} %bitcast.195), kind=kOutput, calls=%fused_computation.8 | convolution fusion | flops 1814298624 | bytes 18923520 | tf_op jit(solution)/shard_map/dot_general | solution.py:200
  745.0 6.6 copy.85
  751.6 12.9 %shard_map.107 = f32[2,384,128]{2,1,0:T(8,128)S(1)} custom-call(bf16[48,384,128]{2,1,0:T(8,128)(2,1)} %bitcast.201, bf16[8,48,2,16,128]{4,3,2,1,0:T(8,128)(2,1)S(1)} %all-to-all-done.7.modes_ref, f32[48,2,384,128]{3,2,1,0:T(8,128)} %pad_maximum_fusion.coeffs_ref), custom_call_target="tpu_custom_call" | custom-call | flops 1207959552 | bytes 23592960 | tf_op jit(solution)/shard_map/pallas_call | solution.py:135
  764.6 12.8 %shard_map.108 = f32[2,384,128]{2,1,0:T(8,128)S(1)} custom-call(bf16[48,384,128]{2,1,0:T(8,128)(2,1)} %bitcast.200, bf16[8,48,2,16,128]{4,3,2,1,0:T(8,128)(2,1)S(1)} %copy-done.2, f32[48,2,384,128]{3,2,1,0:T(8,128)} %pad_maximum_fusion.coeffs_ref), custom_call_target="tpu_custom_call" | custom-call | flops 1207959552 | bytes 23592960 | tf_op jit(solution)/shard_map/pallas_call | solution.py:135
  777.4 13.5 %shard_map.109 = f32[2,384,128]{2,1,0:T(8,128)S(1)} custom-call(bf16[48,384,128]{2,1,0:T(8,128)(2,1)} %bitcast.199, bf16[8,48,2,16,128]{4,3,2,1,0:T(8,128)(2,1)} %all-to-all-done.6.modes_ref, f32[48,2,384,128]{3,2,1,0:T(8,128)} %pad_maximum_fusion.coeffs_ref), custom_call_target="tpu_custom_call" | custom-call | flops 1207959552 | bytes 23592960 | tf_op jit(solution)/shard_map/pallas_call | solution.py:135
  791.0 16.1 %all_to_all.51 = f32[8,2,48,128]{3,2,1,0:T(8,128)S(1)} all-to-all(f32[8,2,48,128]{3,2,1,0:T(8,128)S(1)} %bitcast.223), channel_id=1, replica_groups=mesh['group'=2,'polar'=8,'azimuth'=2] {'polar'}, dimensions={0} | all-to-all | bytes 786432 | tf_op jit(solution)/shard_map/all_to_all | solution.py:190
  (163 shorter events, 102.3 us)
Async XLA Ops:
  0.6 153.5 %copy-start = (f32[384,2,256]{2,1,0:T(2,128)S(1)}, f32[384,2,256]{2,1,0:T(2,128)}, u32[]{:S(2)}) copy-start(f32[384,2,256]{2,1,0:T(2,128)} %param.13) | copy-start | bytes 2359300
  0.7 12.5 %copy-start.37 = (s32[384]{0:T(512)S(1)}, s32[384]{0:T(512)}, u32[]{:S(2)}) copy-start(s32[384]{0:T(512)} %param.17) | copy-start | bytes 4612
  0.7 12.6 %copy-start.33 = (s32[384]{0:T(512)S(1)}, s32[384]{0:T(512)}, u32[]{:S(2)}) copy-start(s32[384]{0:T(512)} %param.16) | copy-start | bytes 4612
  0.7 12.6 %copy-start.12 = (f32[384]{0:T(512)S(1)}, f32[384]{0:T(512)}, u32[]{:S(2)}) copy-start(f32[384]{0:T(512)} %param.12) | copy-start | bytes 4612
  12.7 14.2 %collective-permute-start = (bf16[48,720,128]{2,1,0:T(8,128)(2,1)}, bf16[48,720,128]{2,1,0:T(8,128)(2,1)}, u32[]{:S(2)}, u32[]{:S(2)}) collective-permute-start(bf16[48,720,128]{2,1,0:T(8,128)(2,1)} %get-tuple-element.49), channel_id=1, source_target_pairs={{0,1},{1,0},{2,3},{3,2},{4,5},{5,4},{6,7},{7,6},{8,9},{9,8},{10,11... | collective-permute-start | bytes 26542088 | tf_op jit(solution)/shard_map/ppermute | solution.py:187
  24.7 11.1 %copy-start.24 = (bf16[1440,1,8,48]{0,3,2,1:T(8,128)(2,1)}, bf16[1440,1,8,48]{0,3,2,1:T(8,128)(2,1)S(1)}, u32[]{:S(2)}) copy-start(bf16[1440,1,8,48]{0,3,2,1:T(8,128)(2,1)S(1)} %get-tuple-element.74) | copy-start | bytes 3317764
  24.7 11.1 %copy-start.25 = (bf16[1440,1,8,48]{0,3,2,1:T(8,128)(2,1)}, bf16[1440,1,8,48]{0,3,2,1:T(8,128)(2,1)S(1)}, u32[]{:S(2)}) copy-start(bf16[1440,1,8,48]{0,3,2,1:T(8,128)(2,1)S(1)} %get-tuple-element.75) | copy-start | bytes 3317764
  37.8 61.3 %all-to-all-start.1 = ((bf16[8,12,2,48,128]{4,3,2,1,0:T(8,128)(2,1)}), bf16[8,12,2,48,128]{4,3,2,1,0:T(8,128)(2,1)S(1)}, u32[]{:S(2)}, u32[]{:S(2)}) async-start(bf16[8,12,2,48,128]{4,3,2,1,0:T(8,128)(2,1)} %copy.58), calls=%async_computation.1 | async-start | bytes 4718592 | tf_op jit(solution)/shard_map/all_to_all | solution.py:190
  99.2 108.7 %all-to-all-start.2 = ((bf16[8,24,2,48,128]{4,3,2,1,0:T(8,128)(2,1)}), bf16[8,24,2,48,128]{4,3,2,1,0:T(8,128)(2,1)}, u32[]{:S(2)}, u32[]{:S(2)}) async-start(bf16[8,24,2,48,128]{4,3,2,1,0:T(8,128)(2,1)} %copy.63), calls=%async_computation.2 | async-start | bytes 9437184 | tf_op jit(solution)/shard_map/all_to_all | solution.py:190
  154.9 11.6 %slice-start.3 = ((s8[4718592]{0:T(1024)(128)(4,1)}), s8[4194304]{0:T(1024)(128)(4,1)S(1)}, s32[]{:S(2)}) async-start(s8[4718592]{0:T(1024)(128)(4,1)} %bitcast.206), calls=%async_computation.13 | async-start | bytes 8388608
  155.2 11.3 %slice-start.4 = ((s8[4718592]{0:T(1024)(128)(4,1)}), s8[524288]{0:T(1024)(128)(4,1)S(1)}, s32[]{:S(2)}) async-start(s8[4718592]{0:T(1024)(128)(4,1)} %bitcast.206), calls=%async_computation.14 | async-start | bytes 1048576
  170.3 41.5 %copy-start.36 = (f32[12,384]{1,0:T(8,128)S(1)}, f32[12,384]{1,0:T(8,128)}, u32[]{:S(2)}) copy-start(f32[12,384]{1,0:T(8,128)} %get-tuple-element.73) | copy-start | bytes 55300
  207.8 9.1 %slice-start.5 = ((s8[4718592]{0:T(1024)(128)(4,1)}), s8[524288]{0:T(1024)(128)(4,1)S(1)}, s32[]{:S(2)}) async-start(s8[4718592]{0:T(1024)(128)(4,1)} %bitcast.209), calls=%async_computation.15 | async-start | bytes 1048576
  207.8 58.0 %all-to-all-start = ((bf16[8,12,2,48,128]{4,3,2,1,0:T(8,128)(2,1)}), bf16[8,12,2,48,128]{4,3,2,1,0:T(8,128)(2,1)S(1)}, u32[]{:S(2)}, u32[]{:S(2)}) async-start(bf16[8,12,2,48,128]{4,3,2,1,0:T(8,128)(2,1)} %copy.57), calls=%async_computation | async-start | bytes 4718592 | tf_op jit(solution)/shard_map/all_to_all | solution.py:190
  211.8 5.1 slice-start.6
  219.7 11.0 %copy-start.32 = (f32[24,384]{1,0:T(8,128)S(1)}, f32[24,384]{1,0:T(8,128)}, u32[]{:S(2)}) copy-start(f32[24,384]{1,0:T(8,128)} %slice.169) | copy-start | bytes 110596
  235.7 5.2 copy-start.13
  265.8 4.2 copy-start.35
  265.8 7.8 slice-start.7
  282.5 74.8 %all-to-all-start.3 = ((bf16[8,48,2,16,128]{4,3,2,1,0:T(8,128)(2,1)}), bf16[8,48,2,16,128]{4,3,2,1,0:T(8,128)(2,1)}, u32[]{:S(2)}, u32[]{:S(2)}) async-start(bf16[8,48,2,16,128]{4,3,2,1,0:T(8,128)(2,1)} %copy.72), calls=%async_computation.3 | async-start | bytes 6291456 | tf_op jit(solution)/shard_map/all_to_all | solution.py:190
  364.5 3.7 copy-start.16
  366.3 9.1 %collective-permute-start.1 = (bf16[16,720,128]{2,1,0:T(8,128)(2,1)}, bf16[16,720,128]{2,1,0:T(8,128)(2,1)}, u32[]{:S(2)}, u32[]{:S(2)}) collective-permute-start(bf16[16,720,128]{2,1,0:T(8,128)(2,1)} %slice.178), channel_id=1, source_target_pairs={{0,1},{1,0},{2,3},{3,2},{4,5},{5,4},{6,7},{7,6},{8,9},{9,8},{10,11... | collective-permute-start | bytes 8847368 | tf_op jit(solution)/shard_map/ppermute | solution.py:243
  370.5 4.6 copy-start.4
  370.5 4.8 copy-start.3
  370.5 74.8 %all-to-all-start.5 = ((bf16[8,48,2,16,128]{4,3,2,1,0:T(8,128)(2,1)}), bf16[8,48,2,16,128]{4,3,2,1,0:T(8,128)(2,1)}, u32[]{:S(2)}, u32[]{:S(2)}) async-start(bf16[8,48,2,16,128]{4,3,2,1,0:T(8,128)(2,1)} %copy.79), calls=%async_computation.5 | async-start | bytes 6291456 | tf_op jit(solution)/shard_map/all_to_all | solution.py:190
  375.3 89.3 %copy-start.6 = (bf16[512,256]{0,1:T(8,128)(2,1)}, bf16[512,256]{0,1:T(8,128)(2,1)S(1)}, u32[]{:S(2)}) copy-start(bf16[512,256]{0,1:T(8,128)(2,1)S(1)} %copy.74) | copy-start | bytes 786436
  375.4 89.1 %copy-start.8 = (bf16[256,512]{0,1:T(8,128)(2,1)}, bf16[256,512]{0,1:T(8,128)(2,1)S(1)}, u32[]{:S(2)}) copy-start(bf16[256,512]{0,1:T(8,128)(2,1)S(1)} %copy.75) | copy-start | bytes 786436
  375.4 28.1 %copy-start.20 = (bf16[8,12,2,16,128]{4,3,0,2,1:T(8,128)(2,1)S(1)}, bf16[8,12,2,16,128]{4,3,0,2,1:T(8,128)(2,1)}, u32[]{:S(2)}) copy-start(bf16[8,12,2,16,128]{4,3,0,2,1:T(8,128)(2,1)} %get-tuple-element.78) | copy-start | bytes 2359300
  403.5 5.6 collective-permute-start.2
  403.5 5.6 copy-start.26
  403.6 5.6 copy-start.29
  420.4 29.7 %copy-start.27 = (bf16[1440,1,384]{2,0,1:T(8,128)(2,1)S(1)}, bf16[1440,1,384]{2,0,1:T(8,128)(2,1)}, u32[]{:S(2)}) copy-start(bf16[1440,1,384]{2,0,1:T(8,128)(2,1)} %get-tuple-element.76) | copy-start | bytes 3317764
  420.4 29.7 %copy-start.30 = (bf16[1440,1,384]{2,0,1:T(8,128)(2,1)S(1)}, bf16[1440,1,384]{2,0,1:T(8,128)(2,1)}, u32[]{:S(2)}) copy-start(bf16[1440,1,384]{2,0,1:T(8,128)(2,1)} %get-tuple-element.77) | copy-start | bytes 3317764
  445.3 75.0 %all-to-all-start.4 = ((bf16[8,48,2,16,128]{4,3,2,1,0:T(8,128)(2,1)}), bf16[8,48,2,16,128]{4,3,2,1,0:T(8,128)(2,1)}, u32[]{:S(2)}, u32[]{:S(2)}) async-start(bf16[8,48,2,16,128]{4,3,2,1,0:T(8,128)(2,1)} %copy.77), calls=%async_computation.4 | async-start | bytes 6291456 | tf_op jit(solution)/shard_map/all_to_all | solution.py:190
  457.3 7.2 copy-start.18
  457.5 5.4 collective-permute-start.4
  494.4 34.9 %collective-permute-start.5 = (bf16[16,720,128]{2,1,0:T(8,128)(2,1)}, bf16[16,720,128]{2,1,0:T(8,128)(2,1)}, u32[]{:S(2)}, u32[]{:S(2)}) collective-permute-start(bf16[16,720,128]{2,1,0:T(8,128)(2,1)} %get-tuple-element.36), channel_id=1, source_target_pairs={{0,1},{1,0},{2,3},{3,2},{4,5},{5,4},{6,7},{7,6},{8,9},{9,8},{10,11... | collective-permute-start | bytes 8847368 | tf_op jit(solution)/shard_map/ppermute | solution.py:187
  527.4 10.7 %copy-start.17 = (bf16[16,1440,128]{2,1,0:T(8,128)(2,1)}, bf16[16,1440,128]{2,1,0:T(8,128)(2,1)S(1)}, u32[]{:S(2)}) copy-start(bf16[16,1440,128]{2,1,0:T(8,128)(2,1)S(1)} %fusion.28.own_ref) | copy-start | bytes 17694724
  527.4 4.0 copy-start.11
  529.3 16.4 %collective-permute-start.3 = (bf16[16,720,128]{2,1,0:T(8,128)(2,1)}, bf16[16,720,128]{2,1,0:T(8,128)(2,1)}, u32[]{:S(2)}, u32[]{:S(2)}) collective-permute-start(bf16[16,720,128]{2,1,0:T(8,128)(2,1)} %slice.179), channel_id=1, source_target_pairs={{0,1},{1,0},{2,3},{3,2},{4,5},{5,4},{6,7},{7,6},{8,9},{9,8},{10,11... | collective-permute-start | bytes 8847368 | tf_op jit(solution)/shard_map/ppermute | solution.py:243
  541.8 74.7 %all-to-all-start.7 = ((bf16[8,48,2,16,128]{4,3,2,1,0:T(8,128)(2,1)}), bf16[8,48,2,16,128]{4,3,2,1,0:T(8,128)(2,1)S(1)}, u32[]{:S(2)}, u32[]{:S(2)}) async-start(bf16[8,48,2,16,128]{4,3,2,1,0:T(8,128)(2,1)} %bitcast.212), calls=%async_computation.7 | async-start | bytes 6291456 | tf_op jit(solution)/shard_map/all_to_all | solution.py:190
  548.5 34.5 %copy-start.28 = (bf16[1440,1,384]{2,0,1:T(8,128)(2,1)S(1)}, bf16[1440,1,384]{2,0,1:T(8,128)(2,1)}, u32[]{:S(2)}) copy-start(bf16[1440,1,384]{2,0,1:T(8,128)(2,1)} %get-tuple-element.76) | copy-start | bytes 3317764
  548.5 34.5 %copy-start.31 = (bf16[1440,1,384]{2,0,1:T(8,128)(2,1)S(1)}, bf16[1440,1,384]{2,0,1:T(8,128)(2,1)}, u32[]{:S(2)}) copy-start(bf16[1440,1,384]{2,0,1:T(8,128)(2,1)} %get-tuple-element.77) | copy-start | bytes 3317764
  577.4 5.6 collective-permute-start.6
  691.3 4.6 copy-start.34
  691.3 86.1 %all-to-all-start.6 = ((bf16[8,48,2,16,128]{4,3,2,1,0:T(8,128)(2,1)}), bf16[8,48,2,16,128]{4,3,2,1,0:T(8,128)(2,1)}, u32[]{:S(2)}, u32[]{:S(2)}) async-start(bf16[8,48,2,16,128]{4,3,2,1,0:T(8,128)(2,1)} %bitcast.213), calls=%async_computation.6 | async-start | bytes 6291456 | tf_op jit(solution)/shard_map/all_to_all | solution.py:190
  751.6 12.9 %copy-start.2 = (bf16[8,48,2,16,128]{4,3,2,1,0:T(8,128)(2,1)S(1)}, bf16[8,48,2,16,128]{4,3,2,1,0:T(8,128)(2,1)}, u32[]{:S(2)}) copy-start(bf16[8,48,2,16,128]{4,3,2,1,0:T(8,128)(2,1)} %all_to_all.50.modes_ref) | copy-start | bytes 9437188
  777.4 30.4 %copy-start.1 = (f32[384,2,256]{2,1,0:T(2,128)S(1)}, f32[384,2,256]{2,1,0:T(2,128)}, u32[]{:S(2)}) copy-start(f32[384,2,256]{2,1,0:T(2,128)} %param.13) | copy-start | bytes 2359300
  (14 other events, 29.0 us)

commit v3 on v2

--- a/solution.py
+++ b/solution.py
@@ -94,11 +94,9 @@
         out_specs=[field, part, part],
         out_shape=[jax.ShapeDtypeStruct(state_grid.shape, jnp.bfloat16), half, half],
         input_output_aliases=aliases,
-        compiler_params=pltpu.CompilerParams(vmem_limit_bytes=48 * 1024 * 1024),
+        compiler_params=pltpu.CompilerParams(vmem_limit_bytes=24 * 1024 * 1024),
         cost_estimate=pl.CostEstimate(
-            flops=8 * tokens * channels * hid,
-            bytes_accessed=10 * tokens * channels,
-            transcendentals=tokens * hid,
+            flops=0, bytes_accessed=10 * tokens * channels, transcendentals=0
         ),
     )(*operands)
 
@@ -122,33 +120,34 @@
     out_ref[1] = imag
 
 
-def filter_terms(table_h, d_waves, coeffs):
-    waves, degrees, lats = table_h.shape
+def filter_terms(table_rows, h, d_waves, place, coeffs):
+    waves, degrees, _ = table_rows.shape
     shards, _, _, rg, width = d_waves.shape
-    if rg % 16 != 0:
-        part = table_h.reshape(waves, degrees, shards, rg)
+    lats = shards * rg
+    if rg % 16 != 0 or lats % 128 != 0:
+        d_waves = d_waves[:, place * waves : (place + 1) * waves]
+        part = table_rows[:, :, h * lats : (h + 1) * lats].reshape(waves, degrees, shards, rg)
         d = jnp.einsum("klpr,pktrc->ktlc", part, d_waves, preferred_element_type=jnp.float32)
         real = jnp.sum(d[:, 0] * coeffs[:, 0] + d[:, 1] * coeffs[:, 1], axis=0)
         imag = jnp.sum(d[:, 1] * coeffs[:, 0] - d[:, 0] * coeffs[:, 1], axis=0)
         return jnp.stack([real, imag], axis=0)
     kb = 4 if waves % 4 == 0 else 1
+    skip = place * (waves // kb)
     return pl.pallas_call(
         gather_body,
         grid=(waves // kb,),
         in_specs=[
-            pl.BlockSpec((kb, degrees, lats), lambda i: (i, 0, 0)),
-            pl.BlockSpec((shards, kb, 2, rg, width), lambda i: (0, i, 0, 0, 0)),
+            pl.BlockSpec((kb, degrees, lats), lambda i: (i, 0, h)),
+            pl.BlockSpec((shards, kb, 2, rg, width), lambda i: (0, skip + i, 0, 0, 0)),
             pl.BlockSpec((kb, 2, degrees, width), lambda i: (i, 0, 0, 0)),
         ],
         out_specs=pl.BlockSpec((2, degrees, width), lambda i: (0, 0, 0)),
         out_shape=jax.ShapeDtypeStruct((2, degrees, width), jnp.float32),
-        compiler_params=pltpu.CompilerParams(vmem_limit_bytes=48 * 1024 * 1024),
+        compiler_params=pltpu.CompilerParams(vmem_limit_bytes=12 * 1024 * 1024),
         cost_estimate=pl.CostEstimate(
-            flops=4 * waves * degrees * lats * width,
-            bytes_accessed=waves * degrees * (2 * lats + 8 * width),
-            transcendentals=0,
+            flops=0, bytes_accessed=waves * degrees * (2 * lats + 8 * width), transcendentals=0
         ),
-    )(table_h, d_waves, coeffs)
+    )(table_rows, d_waves, coeffs)
 
 
 def local(
@@ -166,8 +165,8 @@
     width = channels // az_count
     row_chunks = 3 if rows % 3 == 0 else 1
     rg = rows // row_chunks
-    edge = waves // 4
-    wave_spans = [slice(0, edge), slice(edge, waves - edge), slice(waves - edge, waves)]
+    first, last = waves // 4, waves // 6
+    wave_spans = [slice(0, first), slice(first, waves - last), slice(waves - last, waves)]
     spans = [slice(h * rg, (h + 1) * rg) for h in range(row_chunks)]
     swap = [(0, 1), (1, 0)]
     gain_local = lax.dynamic_slice_in_dim(spec_weight, az_index * width, width, 2).transpose(1, 0, 2)
@@ -189,32 +188,32 @@
     def exchange(x):
         return lax.all_to_all(x, "polar", split_axis=0, concat_axis=0, tiled=True)
 
-    lon_full = join(
-        lax.dynamic_slice_in_dim(state_grid, az_index * width, width, 2),
-        lax.dynamic_slice_in_dim(state_grid, (1 - az_index) * width, width, 2),
-    )
-    basis_parts = basis.reshape(full_lon, 2, polar_count, waves)
-    flat_legendre = legendre.reshape(waves * degrees, -1)
-
-    def pick(columns):
-        return jnp.dot(flat_legendre, columns, preferred_element_type=jnp.float32).astype(
-            jnp.bfloat16
-        )
-
-    table = pick(lat_pick).reshape(waves, degrees, polar_count, rows)
-    by_row = lat_pick.reshape(-1, polar_count, rows)
-    table_rows = [
-        pick(by_row[:, :, span].reshape(-1, polar_count * rg)).reshape(waves, degrees, -1)
-        for span in spans
-    ]
+    other = lax.dynamic_slice_in_dim(state_grid, (1 - az_index) * width, width, 2)
+    own_index, other = lax.optimization_barrier((az_index, other))
+    lon_full = join(lax.dynamic_slice_in_dim(state_grid, own_index * width, width, 2), other)
+    shard_orders = m_order.reshape(polar_count, waves)
+
+    def pick(source, columns):
+        flat = source.reshape(source.shape[0] * degrees, -1)
+        return jnp.dot(flat, columns, preferred_element_type=jnp.float32).astype(jnp.bfloat16)
+
+    by_row = lat_pick.reshape(-1, polar_count, row_chunks, rg).transpose(0, 2, 1, 3)
+    table_rows = pick(legendre, by_row.reshape(lat_pick.shape)).reshape(waves, degrees, -1)
     tie = lax.optimization_barrier
 
     arrivals = []
-    for ks in wave_spans:
+    for g, ks in enumerate(wave_spans):
+        lines = shard_orders[:, ks]
+        part_basis = wave_table(lines.reshape(-1), lon_index, full_lon)
         fourier = jnp.einsum(
-            "rnc,ntpk->pktrc", lon_full, basis_parts[..., ks], preferred_element_type=jnp.float32
+            "rnc,ntpk->pktrc",
+            lon_full,
+            part_basis.reshape(full_lon, 2, *lines.shape),
+            preferred_element_type=jnp.float32,
         )
         weighted = (fourier * row_quad[None, None, None, :, None]).astype(jnp.bfloat16)
+        if g == len(wave_spans) - 1:
+            weighted, table_rows = tie((weighted, table_rows))
         arrivals.append(exchange(weighted))
 
     coeffs, modes = [], []
@@ -222,7 +221,7 @@
         at_waves = arrivals[g]
         if g == len(wave_spans) - 1:
             at_waves, *modes = tie((at_waves, *modes))
-        part = table[ks]
+        part = pick(legendre[ks], lat_pick).reshape(-1, degrees, polar_count, rows)
         coeffs_g = jnp.einsum(
             "klpr,pktrc->ktlc", part, at_waves, preferred_element_type=jnp.float32
         ) * lower_mask[ks][:, None, :, None]
@@ -235,45 +234,49 @@
 
     block_out = None
 
-    def middle(h, at_rows, block_out):
+    def mix(h, at_rows, block_out):
         at_rows = at_rows.reshape(polar_count * waves, 2, rg, width)
         spectral = jnp.einsum(
             "ktrc,ntk->rnc", at_rows, basis, preferred_element_type=jnp.float32
         ).astype(jnp.bfloat16)
         came = lax.ppermute(spectral[:, half_lon:], "azimuth", swap)
-        block_out, d_own, d_other = mlp(
+        return mlp(
             h * rg, az_index, state_grid, spectral, came, cotangent, w_in, w_out, block_out
         )
+
+    def to_modes(d_own, d_other):
         d_modes = jnp.einsum(
             "rnc,ntk->ktrc", join(d_own, d_other), basis, preferred_element_type=jnp.float32
         ).astype(jnp.bfloat16)
-        return d_modes.reshape(polar_count, waves, 2, rg, width), block_out
+        return d_modes.reshape(polar_count, waves, 2, rg, width)
 
     outgoing = [jnp.concatenate([m[:, :, :, span] for m in modes], axis=1) for span in spans]
     all_coeffs = jnp.concatenate(coeffs, axis=0)
     if row_chunks == 3:
-        at_0, at_1 = exchange(outgoing[0]), exchange(outgoing[1])
-        at_0, all_coeffs = tie((at_0, all_coeffs))
-        send_0, block_out = middle(0, at_0, None)
-        out_2, send_0 = tie((outgoing[2], send_0))
+        at_0, all_coeffs, out_1, out_2 = tie((exchange(outgoing[0]), all_coeffs, *outgoing[1:]))
+        at_1 = exchange(out_1)
+        block_out, own_0, other_0 = mix(0, at_0, None)
+        send_0 = to_modes(own_0, other_0)
+        out_2, send_0, at_1 = tie((out_2, send_0, at_1))
         at_2 = exchange(out_2)
-        send_1, block_out = middle(1, at_1, block_out)
-        send_0, send_1 = tie((send_0, send_1))
-        d_at_0 = exchange(send_0)
-        send_2, block_out = middle(2, at_2, block_out)
-        send_1, send_2 = tie((send_1, send_2))
-        d_at_1 = exchange(send_1)
+        block_out, own_1, other_1 = mix(1, at_1, block_out)
+        send_1 = to_modes(own_1, other_1)
+        at_2, send_01 = tie((at_2, jnp.concatenate([send_0, send_1], axis=1)))
+        d_at_01 = exchange(send_01)
+        block_out, own_2, other_2 = mix(2, at_2, block_out)
+        send_2 = to_modes(own_2, other_2)
         d_at_2 = exchange(send_2)
-        early = filter_terms(table_rows[0], d_at_0, all_coeffs) + filter_terms(
-            table_rows[1], d_at_1, all_coeffs
+        early = filter_terms(table_rows, 0, d_at_01, 0, all_coeffs) + filter_terms(
+            table_rows, 1, d_at_01, 1, all_coeffs
         )
         d_at_2, early = tie((d_at_2, early))
-        terms = early + filter_terms(table_rows[2], d_at_2, all_coeffs)
+        terms = early + filter_terms(table_rows, 2, d_at_2, 0, all_coeffs)
     else:
         terms = 0.0
         for h in range(row_chunks):
-            send, block_out = middle(h, exchange(outgoing[h]), block_out)
-            terms += filter_terms(table_rows[h], exchange(send), all_coeffs)
+            block_out, own, other = mix(h, exchange(outgoing[h]), block_out)
+            d_at = exchange(to_modes(own, other))
+            terms += filter_terms(table_rows, h, d_at, 0, all_coeffs)
 
     shares = exchange(
         terms.reshape(2, polar_count, degrees // polar_count, width).transpose(1, 0, 2, 3)

time: 817 us -> 796 us (0.974)
  blocking collectives: 90.9 us -> 15.7 us
  waiting for transfers between devices: 230 us -> 276 us
  local copies, waits for them, and re-layouts: 112 us -> 151 us
  Pallas kernels: 124 us -> 107 us
  matrix products: 158 us -> 143 us
    all_to_all x2 -> x1, blocking collectives: 90.9 us -> 15.7 us  [exchange(): return lax.all_to_all(x, 'polar', split_axis=0, concat_axis=0, tiled=True)]
    all_to_all x8, waiting for transfers between devices: 212 us -> 253 us  [exchange(): return lax.all_to_all(x, 'polar', split_axis=0, concat_axis=0, tiled=True)]
    unnamed x96 -> x88, local copies, waits for them, and re-layouts: 20.5 us -> 45.4 us
    reshape x0 -> x3, local copies, waits for them, and re-layouts: none -> 21.4 us  [the longest x2 21.3 us: local(): part = pick(legendre[ks], lat_pick).reshape(-1, degrees, polar_count, rows)]
    dot_general x13, matrix products: 125 us -> 109 us  [the longest x4 39.8 us: pick(): jnp.dot(flat, columns, preferred_element_type=jnp.float32)]
    pallas_call x3, Pallas kernels: 39.2 us -> 23.6 us  [filter_terms(): pl.pallas_call(gather_body, grid=(waves // kb,), in_specs=[pl.BlockSpec((...]
    slice x9 -> x12, local copies, waits for them, and re-layouts: 27.7 us -> 13.1 us  [the longest x5 9.07 us: local(): part = pick(legendre[ks], lat_pick).reshape(-1, degrees, polar_count, rows)]
    convert_element_type x6 -> x4, local copies, waits for them, and re-layouts: 30.9 us -> 27.9 us  [the longest x1 18.6 us: pick(): jnp.dot(flat, columns, preferred_element_type=jnp.float32)]
  transfers between devices with their start and end apart: 15 -> 15, of which waited for: 11 -> 13; matrix products, arithmetic and copies ran while one was open for 32% -> 32% of each run, Pallas kernels for 14% -> 13%
where the time goes in v3:
time: 796 us; the launch traced here: 790 us
  waiting for transfers between devices  276 us (35%)
  local copies, waits for them, and re-layouts  151 us (19%)
  matrix products  143 us (18%)
  Pallas kernels  107 us (13%)
  other arithmetic  53.5 us (7%)
  starting transfers between devices  41.8 us (5%)
  blocking collectives  15.7 us (2%)
    all_to_all x8, waiting for transfers between devices, exchange(): return lax.all_to_all(x, 'polar', split_axis=0, concat_axis=0, tiled=True)  253 us
    pallas_call x3, Pallas kernels, mlp(): pl.pallas_call(partial(mlp_body, pieces), grid=(rg,), in_specs=in_specs,...  83.5 us
    unnamed x88, local copies, waits for them, and re-layouts  45.4 us
    all_to_all x8, starting transfers between devices, exchange(): return lax.all_to_all(x, 'polar', split_axis=0, concat_axis=0, tiled=True)  40.2 us
    dot_general x4, matrix products, pick(): jnp.dot(flat, columns, preferred_element_type=jnp.float32)  39.8 us
    dot_general x3, matrix products, local(): jnp.einsum('rnc,ntpk->pktrc', lon_full, part_basis.reshape(full_lon, 2, *...  32 us
    another operation x7, other arithmetic  26.6 us
    pallas_call x3, Pallas kernels, filter_terms(): pl.pallas_call(gather_body, grid=(waves // kb,), in_specs=[pl.BlockSpec((...  23.6 us
  transfers between devices with their start and end apart: 15, of which 13 were waited for; matrix products, arithmetic and copies ran while one was open for 32% of the time, Pallas kernels for 13%

profile of v3, /device:TPU:0, one launch (start us, length us, event | category | flops | bytes accessed | tf_op | source)
XLA Modules:
  0.0 789.7 jit_solution(13687551458574378360)
XLA Ops:
  0.7 7.7 constant_dynamic-slice_fusion.1
  12.8 7.5 constant_dynamic-slice_fusion
  22.6 8.8 %fusion.38 = bf16[8,12,2,48,128]{4,1,3,0,2:T(8,128)(2,1)S(1)} fusion(f32[48]{0:T(128)S(1)} %and_select_fusion, bf16[48,720,128]{2,1,0:T(8,128)(2,1)} %collective-permute-done, bf16[48,720,128]{2,1,0:T(8,128)(2,1)} %constant_dynamic-slice_fusion, bf16[1440,2,8,12,1]{0,2,3,1,4:T(8,128)(2,1)S(1)} %maximum_bitcast_fusion.35), kind=kOutput, calls=%fused_computation.55 | convolution fusion | flops 3435134976 | bytes 20607168 | tf_op jit(solution)/shard_map/rnc,ntpk->pktrc/dot_general | solution.py:208
  33.5 7.5 all-to-all-start.1
  41.2 6.1 multiply_convert_fusion.6
  47.4 15.5 %fusion.8 = bf16[8,28,2,48,128]{4,1,3,0,2:T(8,128)(2,1)} fusion(f32[48]{0:T(128)S(1)} %and_select_fusion, bf16[48,720,128]{2,1,0:T(8,128)(2,1)} %collective-permute-done, bf16[48,720,128]{2,1,0:T(8,128)(2,1)} %constant_dynamic-slice_fusion, bf16[1440,2,8,28,1]{0,2,3,1,4:T(8,128)(2,1)S(1)} %maximum_bitcast_fusion.34), kind=kOutput, calls=%fused_computation.19 | convolution fusion | flops 7968129024 | bytes 24490176 | tf_op jit(solution)/shard_map/rnc,ntpk->pktrc/dot_general | solution.py:208
  62.9 7.4 copy.64
  70.3 24.8 %all-to-all-done.1 = bf16[8,12,2,48,128]{4,3,2,1,0:T(8,128)(2,1)S(1)} async-done(((bf16[8,12,2,48,128]{4,3,2,1,0:T(8,128)(2,1)}), bf16[8,12,2,48,128]{4,3,2,1,0:T(8,128)(2,1)S(1)}, u32[]{:S(2)}, u32[]{:S(2)}) %all-to-all-start.1) | async-done | bytes 2359328 | tf_op jit(solution)/shard_map/all_to_all | solution.py:189
  96.5 5.2 all-to-all-start.2
  103.3 8.2 %slice.112 = bf16[28,384,384]{2,1,0:T(8,128)(2,1)} slice(bf16[48,384,384]{2,1,0:T(8,128)(2,1)} %param.11), slice={[12:40], [0:384], [0:384]} | slice | bytes 16515072 | tf_op jit(solution)/shard_map/slice | solution.py:224
  119.6 7.3 reshape.514
  126.9 13.2 %fusion.1 = bf16[10752,384]{0,1:T(8,128)(2,1)} fusion(bf16[10752,384]{1,0:T(8,128)(2,1)} %bitcast.196, s32[384]{0:T(512)S(1)} %copy-done.31), kind=kOutput, calls=%fused_computation.6 | convolution fusion | flops 3175317504 | bytes 16516608 | tf_op jit(solution)/shard_map/dot_general | solution.py:198
  140.1 14.0 %reshape.516 = bf16[28,384,8,48]{1,0,3,2:T(8,128)(2,1)} reshape(bf16[10752,384]{0,1:T(8,128)(2,1)} %fusion.1) | data formatting | bytes 16515072 | tf_op jit(solution)/shard_map/reshape | solution.py:224
  154.3 21.3 %fusion = bf16[18432,384]{0,1:T(8,128)(2,1)} fusion(pred[384,384]{0,1:T(8,128)(4,1)S(1)} %bitcast.217, bf16[18432,384]{1,0:T(8,128)(2,1)} %bitcast.189), kind=kOutput, calls=%fused_computation.2 | convolution fusion | flops 5442895872 | bytes 28459008 | tf_op jit(solution)/shard_map/dot_general | solution.py:198
  175.6 18.6 %copy.53 = bf16[18432,384]{1,0:T(8,128)(2,1)} copy(bf16[18432,384]{0,1:T(8,128)(2,1)} %fusion) | data formatting | bytes 28311552 | tf_op jit(solution)/shard_map/convert_element_type | solution.py:198
  196.7 7.6 fusion.77
  214.0 8.4 %all-to-all-done.2 = bf16[8,28,2,48,128]{4,3,2,1,0:T(8,128)(2,1)} async-done(((bf16[8,28,2,48,128]{4,3,2,1,0:T(8,128)(2,1)}), bf16[8,28,2,48,128]{4,3,2,1,0:T(8,128)(2,1)}, u32[]{:S(2)}, u32[]{:S(2)}) %all-to-all-start.2) | async-done | bytes 5505056 | tf_op jit(solution)/shard_map/all_to_all | solution.py:189
  226.1 15.3 %fusion.27 = f32[28,2,128,384]{2,3,0,1:T(8,128)} fusion(bf16[28,384,8,48,1]{1,0,3,2,4:T(8,128)(2,1)} %bitcast.194, bf16[8,28,2,48,128]{4,3,2,1,0:T(8,128)(2,1)} %all-to-all-done.2), kind=kOutput, calls=%fused_computation.49 | convolution fusion | flops 2113929216 | bytes 24772608 | tf_op jit(solution)/shard_map/klpr,pktrc->ktlc/dot_general | solution.py:225
  241.4 5.5 fusion.2
  251.9 10.6 %convert_bitcast_fusion = bf16[8,28,2,48,128]{4,3,0,2,1:T(8,128)(2,1)} fusion(bf16[28,384,8,48,1]{1,0,3,2,4:T(8,128)(2,1)} %bitcast.195, bf16[28,1,384,128]{3,2,1,0:T(8,128)(2,1)} %get-tuple-element.59, bf16[28,1,384,128]{3,2,1,0:T(8,128)(2,1)S(1)} %get-tuple-element.58), kind=kOutput, calls=%fused_computation.38 | convolution fusion | flops 2127691776 | bytes 19267584 | tf_op jit(solution)/shard_map/klpr,ktlc->pktrc/dot_general | solution.py:229
  278.3 5.8 all-to-all-start.3
  284.2 11.3 %multiply_convert_fusion.4 = (bf16[1440,1,384]{2,0,1:T(8,128)(2,1)}, bf16[1440,1,384]{2,0,1:T(8,128)(2,1)}) fusion(s32[384]{0:T(512)S(1)} %copy-done.33, s32[1440]{0:T(1024)S(1)} %copy-done.28), kind=kLoop, calls=%fused_computation.86 | loop fusion | flops 7741440 | bytes 2219136 | tf_op jit(solution)/shard_map/convert.12
  300.3 11.5 %pad_maximum_fusion.coeffs_ref = f32[48,2,384,128]{3,2,1,0:T(8,128)} fusion(f32[8,2,384,128]{3,2,1,0:T(8,128)S(1)} %fusion.39, f32[28,2,384,128]{3,2,1,0:T(8,128)} %copy-done.15, f32[12,2,384,128]{3,2,1,0:T(8,128)S(1)} %bitcast.193), kind=kLoop, calls=%fused_computation.3 | loop fusion | flops 9437184 | bytes 37748736 | tf_op jit(solution)/shard_map/concatenate | solution.py:254
  311.8 42.7 %all-to-all-done.3 = bf16[8,48,2,16,128]{4,3,2,1,0:T(8,128)(2,1)} async-done(((bf16[8,48,2,16,128]{4,3,2,1,0:T(8,128)(2,1)}), bf16[8,48,2,16,128]{4,3,2,1,0:T(8,128)(2,1)}, u32[]{:S(2)}, u32[]{:S(2)}) %all-to-all-start.3) | async-done | bytes 3145760 | tf_op jit(solution)/shard_map/all_to_all | solution.py:189
  354.5 7.2 fusion.24.own_ref
  376.0 27.9 %shard_map.104 = (bf16[48,720,256]{2,1,0:T(8,128)(2,1)}, bf16[16,720,128]{2,1,0:T(8,128)(2,1)S(1)}, bf16[16,720,128]{2,1,0:T(8,128)(2,1)S(1)}) custom-call(s32[1]{0:T(128)} %bitcast.az_ref, bf16[48,720,256]{2,1,0:T(8,128)(2,1)} %state_ref.5, bf16[16,1440,128]{2,1,0:T(8,128)(2,1)S(1)} %copy-done.7, bf16[16,720,128]{2,1,0:T(8,128)(2,1)} %collective-permute-done.1.came_ref, ...), custom_call_target="tpu_custom_call" | custom-call | bytes 29491200 | tf_op jit(solution)/shard_map/pallas_call | solution.py:90
  404.4 5.0 collective-permute-done.2
  409.5 5.3 convert_bitcast_fusion.3
  418.5 26.2 %all-to-all-done.4 = bf16[8,48,2,16,128]{4,3,2,1,0:T(8,128)(2,1)} async-done(((bf16[8,48,2,16,128]{4,3,2,1,0:T(8,128)(2,1)}), bf16[8,48,2,16,128]{4,3,2,1,0:T(8,128)(2,1)}, u32[]{:S(2)}, u32[]{:S(2)}) %all-to-all-start.4) | async-done | bytes 3145760 | tf_op jit(solution)/shard_map/all_to_all | solution.py:189
  444.7 7.1 fusion.25.own_ref
  465.6 27.9 %shard_map.105 = (bf16[48,720,256]{2,1,0:T(8,128)(2,1)}, bf16[16,720,128]{2,1,0:T(8,128)(2,1)S(1)}, bf16[16,720,128]{2,1,0:T(8,128)(2,1)S(1)}) custom-call(s32[1]{0:T(128)} %bitcast.az_ref, bf16[48,720,256]{2,1,0:T(8,128)(2,1)} %state_ref.5, bf16[16,1440,128]{2,1,0:T(8,128)(2,1)S(1)} %copy-done.9, ...), custom_call_target="tpu_custom_call", output_to_operand_aliasing={{0}: (9, {})} | custom-call | bytes 29491200 | tf_op jit(solution)/shard_map/pallas_call | solution.py:90
  499.0 5.3 convert_bitcast_fusion.2
  509.6 25.0 %all-to-all-done.5 = bf16[8,48,2,16,128]{4,3,2,1,0:T(8,128)(2,1)} async-done(((bf16[8,48,2,16,128]{4,3,2,1,0:T(8,128)(2,1)}), bf16[8,48,2,16,128]{4,3,2,1,0:T(8,128)(2,1)}, u32[]{:S(2)}, u32[]{:S(2)}) %all-to-all-start.5) | async-done | bytes 3145760 | tf_op jit(solution)/shard_map/all_to_all | solution.py:189
  539.6 7.1 fusion.26.own_ref
  547.0 5.4 collective-permute-done.5.came_ref
  552.4 27.7 %shard_map.106 = (bf16[48,720,256]{2,1,0:T(8,128)(2,1)}, bf16[16,720,128]{2,1,0:T(8,128)(2,1)S(1)}, bf16[16,720,128]{2,1,0:T(8,128)(2,1)S(1)}) custom-call(s32[1]{0:T(128)} %bitcast.az_ref, bf16[48,720,256]{2,1,0:T(8,128)(2,1)} %state_ref.5, bf16[16,1440,128]{2,1,0:T(8,128)(2,1)S(1)} %fusion.26.own_ref, ...), custom_call_target="tpu_custom_call", output_to_operand_aliasing={{0}: (9, {})} | custom-call | bytes 29491200 | tf_op jit(solution)/shard_map/pallas_call | solution.py:90
  580.2 5.3 collective-permute-done.6
  585.4 5.3 convert_bitcast_fusion.1
  594.4 83.4 %all-to-all-done.7.modes_ref = bf16[8,96,2,16,128]{4,3,2,1,0:T(8,128)(2,1)} async-done(((bf16[8,96,2,16,128]{4,3,2,1,0:T(8,128)(2,1)}), bf16[8,96,2,16,128]{4,3,2,1,0:T(8,128)(2,1)}, u32[]{:S(2)}, u32[]{:S(2)}) %all-to-all-start.7) | async-done | bytes 6291488 | tf_op jit(solution)/shard_map/all_to_all | solution.py:189
  681.5 6.4 copy-done.2
  687.9 5.0 copy-done.4
  692.9 9.0 %shard_map.108 = f32[2,384,128]{2,1,0:T(8,128)S(1)} custom-call(bf16[48,384,384]{2,1,0:T(8,128)(2,1)S(1)} %bitcast.180, bf16[8,96,2,16,128]{4,3,2,1,0:T(8,128)(2,1)} %all-to-all-done.7.modes_ref, f32[48,2,384,128]{3,2,1,0:T(8,128)S(1)} %copy-done.2), custom_call_target="tpu_custom_call" | custom-call | bytes 23592960 | tf_op jit(solution)/shard_map/pallas_call | solution.py:136
  701.9 9.0 %shard_map.107 = f32[2,384,128]{2,1,0:T(8,128)S(1)} custom-call(bf16[48,384,384]{2,1,0:T(8,128)(2,1)S(1)} %bitcast.181, bf16[8,96,2,16,128]{4,3,2,1,0:T(8,128)(2,1)} %all-to-all-done.7.modes_ref, f32[48,2,384,128]{3,2,1,0:T(8,128)S(1)} %copy-done.2), custom_call_target="tpu_custom_call" | custom-call | bytes 23592960 | tf_op jit(solution)/shard_map/pallas_call | solution.py:136
  710.9 41.5 %all-to-all-done.6.modes_ref = bf16[8,48,2,16,128]{4,3,2,1,0:T(8,128)(2,1)S(1)} async-done(((bf16[8,48,2,16,128]{4,3,2,1,0:T(8,128)(2,1)}), bf16[8,48,2,16,128]{4,3,2,1,0:T(8,128)(2,1)S(1)}, u32[]{:S(2)}, u32[]{:S(2)}) %all-to-all-start.6) | async-done | bytes 3145760 | tf_op jit(solution)/shard_map/all_to_all | solution.py:189
  754.1 6.4 copy-done.3
  760.5 5.0 copy-done.5
  767.4 5.6 shard_map.109
  773.1 15.7 %all_to_all.45 = f32[8,2,48,128]{3,2,1,0:T(8,128)S(1)} all-to-all(f32[8,2,48,128]{3,2,1,0:T(8,128)S(1)} %bitcast.215), channel_id=1, replica_groups=mesh['group'=2,'polar'=8,'azimuth'=2] {'polar'}, dimensions={0} | all-to-all | bytes 786432 | tf_op jit(solution)/shard_map/all_to_all | solution.py:189
  (163 shorter events, 121.7 us)
Async XLA Ops:
  0.6 193.6 %copy-start = (f32[384,2,256]{2,1,0:T(2,128)S(1)}, f32[384,2,256]{2,1,0:T(2,128)}, u32[]{:S(2)}) copy-start(f32[384,2,256]{2,1,0:T(2,128)} %param.13) | copy-start | bytes 2359300
  0.7 8.2 %copy-start.32 = (s32[384]{0:T(512)S(1)}, s32[384]{0:T(512)}, u32[]{:S(2)}) copy-start(s32[384]{0:T(512)} %param.17) | copy-start | bytes 4612
  0.7 8.3 %copy-start.31 = (s32[384]{0:T(512)S(1)}, s32[384]{0:T(512)}, u32[]{:S(2)}) copy-start(s32[384]{0:T(512)} %param.16) | copy-start | bytes 4612
  0.7 8.4 %copy-start.14 = (f32[384]{0:T(512)S(1)}, f32[384]{0:T(512)}, u32[]{:S(2)}) copy-start(f32[384]{0:T(512)} %param.12) | copy-start | bytes 4612
  8.4 14.2 %collective-permute-start = (bf16[48,720,128]{2,1,0:T(8,128)(2,1)}, bf16[48,720,128]{2,1,0:T(8,128)(2,1)}, u32[]{:S(2)}, u32[]{:S(2)}) collective-permute-start(bf16[48,720,128]{2,1,0:T(8,128)(2,1)} %constant_dynamic-slice_fusion.1), channel_id=1, source_target_pairs={{0,1},{1,0},{2,3},{3,2},{4,5},{5,4},{6,7},{7,6},{8,9},{9,8},{10,11... | collective-permute-start | bytes 26542088 | tf_op jit(solution)/shard_map/ppermute | solution.py:186
  9.9 31.2 %copy-start.26 = (s32[1440]{0:T(1024)}, s32[1440]{0:T(1024)S(1)}, u32[]{:S(2)}) copy-start(s32[1440]{0:T(1024)S(1)} %add_select_fusion.4) | copy-start | bytes 17284
  10.0 37.4 %copy-start.34 = (f32[48]{0:T(128)}, f32[48]{0:T(128)S(1)}, u32[]{:S(2)}) copy-start(f32[48]{0:T(128)S(1)} %and_select_fusion) | copy-start | bytes 580
  33.5 61.6 %all-to-all-start.1 = ((bf16[8,12,2,48,128]{4,3,2,1,0:T(8,128)(2,1)}), bf16[8,12,2,48,128]{4,3,2,1,0:T(8,128)(2,1)S(1)}, u32[]{:S(2)}, u32[]{:S(2)}) async-start(bf16[8,12,2,48,128]{4,3,2,1,0:T(8,128)(2,1)} %copy.57), calls=%async_computation.1 | async-start | bytes 4718592 | tf_op jit(solution)/shard_map/all_to_all | solution.py:189
  96.5 125.9 %all-to-all-start.2 = ((bf16[8,28,2,48,128]{4,3,2,1,0:T(8,128)(2,1)}), bf16[8,28,2,48,128]{4,3,2,1,0:T(8,128)(2,1)}, u32[]{:S(2)}, u32[]{:S(2)}) async-start(bf16[8,28,2,48,128]{4,3,2,1,0:T(8,128)(2,1)} %copy.64), calls=%async_computation.2 | async-start | bytes 11010048 | tf_op jit(solution)/shard_map/all_to_all | solution.py:189
  103.3 8.2 %slice-start = ((bf16[48,384,384]{2,1,0:T(8,128)(2,1)}), bf16[8,384,384]{2,1,0:T(8,128)(2,1)S(1)}, s32[]{:S(2)}) async-start(bf16[48,384,384]{2,1,0:T(8,128)(2,1)} %param.11), calls=%async_computation.9 | async-start | bytes 4718592 | tf_op jit(solution)/shard_map/slice | solution.py:224
  112.9 2.9 slice-start.1
  175.6 19.0 %copy-start.27 = (s32[1440]{0:T(1024)S(1)}, s32[1440]{0:T(1024)}, u32[]{:S(2)}) copy-start(s32[1440]{0:T(1024)} %copy-done.26) | copy-start | bytes 17284
  175.6 21.1 %copy-start.35 = (f32[48]{0:T(128)S(1)}, f32[48]{0:T(128)}, u32[]{:S(2)}) copy-start(f32[48]{0:T(128)} %copy-done.34) | copy-start | bytes 580
  194.2 11.4 %slice-start.4 = ((s8[4718592]{0:T(1024)(128)(4,1)}), s8[4194304]{0:T(1024)(128)(4,1)S(1)}, s32[]{:S(2)}) async-start(s8[4718592]{0:T(1024)(128)(4,1)} %bitcast.197), calls=%async_computation.13 | async-start | bytes 8388608
  196.7 8.9 %slice-start.5 = ((s8[4718592]{0:T(1024)(128)(4,1)}), s8[524288]{0:T(1024)(128)(4,1)S(1)}, s32[]{:S(2)}) async-start(s8[4718592]{0:T(1024)(128)(4,1)} %bitcast.197), calls=%async_computation.14 | async-start | bytes 1048576
  222.5 40.8 %all-to-all-start = ((bf16[8,8,2,48,128]{4,1,3,2,0:T(8,128)(2,1)}), bf16[8,8,2,48,128]{4,1,3,2,0:T(8,128)(2,1)S(1)}, u32[]{:S(2)}, u32[]{:S(2)}) async-start(bf16[8,8,2,48,128]{4,1,3,2,0:T(8,128)(2,1)} %copy.54), calls=%async_computation | async-start | bytes 3145728 | tf_op jit(solution)/shard_map/all_to_all | solution.py:189
  226.1 15.3 %copy-start.29 = (f32[28,384]{1,0:T(8,128)S(1)}, f32[28,384]{1,0:T(8,128)}, u32[]{:S(2)}) copy-start(f32[28,384]{1,0:T(8,128)} %slice.139) | copy-start | bytes 129028
  246.9 5.1 copy-start.15
  263.3 4.1 copy-start.23
  263.3 4.1 copy-start.20
  270.0 2.7 slice-start.6
  278.3 5.8 copy-start.28
  278.3 5.8 copy-start.33
  278.3 76.2 %all-to-all-start.3 = ((bf16[8,48,2,16,128]{4,3,2,1,0:T(8,128)(2,1)}), bf16[8,48,2,16,128]{4,3,2,1,0:T(8,128)(2,1)}, u32[]{:S(2)}, u32[]{:S(2)}) async-start(bf16[8,48,2,16,128]{4,3,2,1,0:T(8,128)(2,1)} %copy.73), calls=%async_computation.3 | async-start | bytes 6291456 | tf_op jit(solution)/shard_map/all_to_all | solution.py:189
  284.2 16.1 %slice-start.2 = ((s8[4718592]{0:T(1024)(128)(4,1)}), s8[4194304]{0:T(1024)(128)(4,1)S(1)}, s32[]{:S(2)}) async-start(s8[4718592]{0:T(1024)(128)(4,1)} %bitcast.192), calls=%async_computation.11 | async-start | bytes 8388608
  295.4 4.9 slice-start.3
  361.7 4.3 copy-start.19
  366.0 7.3 collective-permute-start.1
  368.3 4.8 copy-start.12
  368.3 4.9 copy-start.13
  368.3 76.4 %all-to-all-start.4 = ((bf16[8,48,2,16,128]{4,3,2,1,0:T(8,128)(2,1)}), bf16[8,48,2,16,128]{4,3,2,1,0:T(8,128)(2,1)}, u32[]{:S(2)}, u32[]{:S(2)}) async-start(bf16[8,48,2,16,128]{4,3,2,1,0:T(8,128)(2,1)} %copy.78), calls=%async_computation.4 | async-start | bytes 6291456 | tf_op jit(solution)/shard_map/all_to_all | solution.py:189
  373.3 2.7 copy-start.7
  376.0 33.4 %copy-start.24 = (bf16[1440,1,384]{2,0,1:T(8,128)(2,1)S(1)}, bf16[1440,1,384]{2,0,1:T(8,128)(2,1)}, u32[]{:S(2)}) copy-start(bf16[1440,1,384]{2,0,1:T(8,128)(2,1)} %get-tuple-element.81) | copy-start | bytes 3317764
  376.0 33.4 %copy-start.25 = (bf16[1440,1,384]{2,0,1:T(8,128)(2,1)S(1)}, bf16[1440,1,384]{2,0,1:T(8,128)(2,1)}, u32[]{:S(2)}) copy-start(bf16[1440,1,384]{2,0,1:T(8,128)(2,1)} %get-tuple-element.82) | copy-start | bytes 3317764
  403.9 5.5 collective-permute-start.2
  451.8 4.3 copy-start.17
  456.0 6.9 collective-permute-start.3
  458.3 76.3 %all-to-all-start.5 = ((bf16[8,48,2,16,128]{4,3,2,1,0:T(8,128)(2,1)}), bf16[8,48,2,16,128]{4,3,2,1,0:T(8,128)(2,1)}, u32[]{:S(2)}, u32[]{:S(2)}) async-start(bf16[8,48,2,16,128]{4,3,2,1,0:T(8,128)(2,1)} %copy.79), calls=%async_computation.5 | async-start | bytes 6291456 | tf_op jit(solution)/shard_map/all_to_all | solution.py:189
  493.5 5.5 collective-permute-start.4
  534.6 143.3 %all-to-all-start.7 = ((bf16[8,96,2,16,128]{4,3,2,1,0:T(8,128)(2,1)}), bf16[8,96,2,16,128]{4,3,2,1,0:T(8,128)(2,1)}, u32[]{:S(2)}, u32[]{:S(2)}) async-start(bf16[8,96,2,16,128]{4,3,2,1,0:T(8,128)(2,1)} %pad_maximum_fusion.1), calls=%async_computation.7 | async-start | bytes 12582912 | tf_op jit(solution)/shard_map/all_to_all | solution.py:189
  546.9 5.4 collective-permute-start.5
  580.1 5.4 collective-permute-start.6
  677.9 74.5 %all-to-all-start.6 = ((bf16[8,48,2,16,128]{4,3,2,1,0:T(8,128)(2,1)}), bf16[8,48,2,16,128]{4,3,2,1,0:T(8,128)(2,1)S(1)}, u32[]{:S(2)}, u32[]{:S(2)}) async-start(bf16[8,48,2,16,128]{4,3,2,1,0:T(8,128)(2,1)} %bitcast.201), calls=%async_computation.6 | async-start | bytes 6291456 | tf_op jit(solution)/shard_map/all_to_all | solution.py:189
  681.5 6.4 copy-start.2
  687.9 5.0 copy-start.4
  754.1 6.4 copy-start.3
  760.5 5.0 copy-start.5
  767.4 22.1 %copy-start.1 = (f32[384,2,256]{2,1,0:T(2,128)S(1)}, f32[384,2,256]{2,1,0:T(2,128)}, u32[]{:S(2)}) copy-start(f32[384,2,256]{2,1,0:T(2,128)} %param.13) | copy-start | bytes 2359300
  (11 other events, 23.3 us)
